TPU v7x, 512 devices: a whole 4x8x8 slice. The times are simulated.
512 devices in a mesh: section: 32 (over y, z_hi), dp: 16 (over x, z_lo, core).
Axes of the slice: x: 4, y: 8, z: 8 (z_hi: 4, z_lo: 2; z = z_hi * 2 + z_lo), core: 2. Of those that a mesh axis runs over, the one named last changes fastest.
Arguments:
- inputs: bfloat16 [768, 8192], P(None, 'dp'), may hold values from -6 to 6
- out_grad: bfloat16 [768, 8192], P(None, 'dp'), may hold values from -6 to 6
- saved_codes: int32 [768, 32768], P('dp', 'section'), may hold values from -127 to 127
- row_scale: float32 [768], P('dp'), may hold values from 0.005 to 0.04
- w_in: bfloat16 [8192, 32768], P('dp', 'section'), may hold values from -0.0625 to 0.0625
- w_out: bfloat16 [32768, 8192], P('section', 'dp'), may hold values from -0.03125 to 0.03125
Outputs:
- input_grad: bfloat16 [768, 8192], P('section', 'dp')
- w_in_grad: bfloat16 [8192, 32768], P('dp', 'section')
- w_out_grad: bfloat16 [32768, 8192], P('section', 'dp')
All inputs are finite; a program needn't handle non-finite values.
Results may differ from a plain program's by a relative error of at most 0.015.
Values may be sent and summed in bfloat16 or wider, within the bound.
No kernel may reach another device: no remote copies, remote signals or barrier semaphores. Data moves between devices by JAX's collectives and lax.ppermute only.
A program may use at most 64 MiB of HBM per device.

v0:
```python
import math

import jax
import jax.numpy as jnp
from jax import lax
from jax.sharding import PartitionSpec as P

inv_root_two = 1.0 / math.sqrt(2.0)
inv_root_tau = 1.0 / math.sqrt(2.0 * math.pi)


def contract_last(left, right):
    return lax.dot_general(
        left, right, (((1,), (1,)), ((), ())), preferred_element_type=jnp.float32
    )


def contract_first(left, right):
    return lax.dot_general(
        left, right, (((0,), (0,)), ((), ())), preferred_element_type=jnp.float32
    )


def body(inputs, out_grad, saved_codes, row_scale, w_in, w_out):
    pre_act = saved_codes.astype(jnp.float32) * row_scale[:, None]
    normal_cdf = 0.5 * (1.0 + jax.scipy.special.erf(pre_act * inv_root_two))
    hidden_own = (pre_act * normal_cdf).astype(jnp.bfloat16)
    slope_own = (normal_cdf + pre_act * jnp.exp(-0.5 * pre_act * pre_act) * inv_root_tau).astype(
        jnp.bfloat16
    )
    grad_rows = out_grad
    grad_share = lax.psum_scatter(
        contract_last(grad_rows, w_out), "dp", scatter_dimension=0, tiled=True
    )
    pre_grad_own = (grad_share * slope_own).astype(jnp.bfloat16)
    grad_rows = out_grad
    w_out_total = contract_first(lax.all_gather(hidden_own, "dp", axis=0, tiled=True), grad_rows)
    pre_grad = lax.all_gather(pre_grad_own, "dp", axis=0, tiled=True)
    w_in_total = contract_first(inputs, pre_grad)
    input_grad = lax.psum_scatter(
        contract_last(pre_grad, w_in), "section", scatter_dimension=0, tiled=True
    )
    return (
        input_grad.astype(jnp.bfloat16),
        w_in_total.astype(jnp.bfloat16),
        w_out_total.astype(jnp.bfloat16),
    )


def solution(mesh):
    placed = (
        P(None, "dp"),
        P(None, "dp"),
        P("dp", "section"),
        P("dp"),
        P("dp", "section"),
        P("section", "dp"),
    )
    return jax.shard_map(
        body,
        mesh=mesh,
        in_specs=placed,
        out_specs=(P("section", "dp"), P("dp", "section"), P("section", "dp")),
        check_vma=False,
    )
```

profile of v0, /device:TPU:1, one launch (start us, length us, event | category | flops | bytes accessed | tf_op | source)
XLA Modules:
  0.0 405.9 jit_solution(5500670043068835639)
XLA Ops:
  7.2 0.0 copy-start
  7.2 0.0 reduce-scatter.3.cloned.1.call-start
  7.2 1.2 copy-done
  8.4 3.8 fusion.6
  12.2 0.0 reduce-scatter.3.cloned.1.call-update
  12.2 0.0 all-gather.3.cloned.1.call-start
  12.3 75.4 %reduce-scatter.3.cloned.1.call-done = f32[48,1024]{1,0:T(8,128)} async-done(((f32[768,1024]{1,0:T(8,128)}), f32[48,1024]{1,0:T(8,128)}) %reduce-scatter.3.cloned.1.call-update) | async-done | bytes 196624 | tf_op jit(solution)/shard_map/reduce_scatter | solution.py:32
  87.7 0.0 copy-done.2
  87.7 1.8 multiply_convert_fusion
  89.5 0.0 all-gather.3.cloned.1.call-update
  89.5 0.0 all-gather.5.cloned.1.call-start
  89.6 0.7 all-gather.5.cloned.1.call-update
  90.2 0.0 reduce-scatter.5.cloned.1.call-start
  90.3 40.1 %all-gather.3.cloned.1.call-done = bf16[768,1024]{1,0:T(8,128)(2,1)} async-done(((bf16[48,1024]{1,0:T(8,128)(2,1)}), bf16[768,1024]{1,0:T(8,128)(2,1)}) %all-gather.3.cloned.1.call-update) | async-done | bytes 1572880 | tf_op jit(solution)/shard_map/all_gather | solution.py:38
  130.4 3.6 fusion.7
  134.0 0.0 reduce-scatter.5.cloned.1.call-update
  134.0 1.1 copy-done.5
  135.1 2.4 fusion
  137.6 0.0 copy-start.1
  137.6 1.3 copy.9
  138.9 32.8 %all-gather.5.cloned.1.call-done = bf16[768,1024]{1,0:T(8,128)(2,1)} async-done(((bf16[48,1024]{1,0:T(8,128)(2,1)}), bf16[768,1024]{1,0:T(8,128)(2,1)}) %all-gather.5.cloned.1.call-update) | async-done | bytes 1572880 | tf_op jit(solution)/shard_map/all_gather | solution.py:37
  171.7 3.4 convolution_convert_fusion
  175.1 222.8 %reduce-scatter.5.cloned.1.call-done = f32[24,512]{1,0:T(8,128)} async-done(((f32[768,512]{1,0:T(8,128)}), f32[24,512]{1,0:T(8,128)}) %reduce-scatter.5.cloned.1.call-update) | async-done | bytes 49168 | tf_op jit(solution)/shard_map/reduce_scatter | solution.py:40
  398.0 1.4 convert_element_type.31
  (7 shorter events, 0.0 us)
Async XLA Ops:
  7.2 1.2 copy-start
  7.2 80.5 %reduce-scatter.3.cloned.1.call-start = ((), (), s32[]{:S(2)}) async-start(), calls=%async_computation.2 | async-start | bytes 3342336 | tf_op jit(solution)/shard_map/reduce_scatter | solution.py:32
  12.2 75.5 %copy-start.2 = (s32[48,1024]{1,0:T(8,128)S(1)}, s32[48,1024]{1,0:T(8,128)}, u32[]{:S(2)}) copy-start(s32[48,1024]{1,0:T(8,128)} %param.8) | copy-start | bytes 589828
  12.2 75.5 %copy-start.3 = (f32[48]{0:T(128)S(1)}, f32[48]{0:T(128)}, u32[]{:S(2)}) copy-start(f32[48]{0:T(128)} %param.9) | copy-start | bytes 580
  12.2 118.2 %copy-start.4 = (bf16[512,1024]{1,0:T(8,128)(2,1)S(1)}, bf16[512,1024]{1,0:T(8,128)(2,1)}, u32[]{:S(2)}) copy-start(bf16[512,1024]{1,0:T(8,128)(2,1)} %param.10) | copy-start | bytes 3145732
  12.2 118.2 %all-gather.3.cloned.1.call-start = ((), (), s32[]{:S(2)}) async-start(), calls=%async_computation.3 | async-start | bytes 1671168 | tf_op jit(solution)/shard_map/all_gather | solution.py:38
  89.5 82.2 %all-gather.5.cloned.1.call-start = ((), (), s32[]{:S(2)}) async-start(), calls=%async_computation.5 | async-start | bytes 1671168 | tf_op jit(solution)/shard_map/all_gather | solution.py:37
  90.2 307.7 %reduce-scatter.5.cloned.1.call-start = ((), (), s32[]{:S(2)}) async-start(), calls=%async_computation.4 | async-start | bytes 1622016 | tf_op jit(solution)/shard_map/reduce_scatter | solution.py:40
  134.0 1.1 copy-start.5
  137.6 34.1 %copy-start.1 = (bf16[768,512]{1,0:T(8,128)(2,1)S(1)}, bf16[768,512]{1,0:T(8,128)(2,1)}, u32[]{:S(2)}) copy-start(bf16[768,512]{1,0:T(8,128)(2,1)} %param.7) | copy-start | bytes 2359300
Sparse Core Ops, SparseCore 0:
  12.3 75.3 reduce-scatter.2
  90.4 39.9 all-gather.2
  133.1 38.5 all-gather.4
  176.0 221.8 reduce-scatter.4
where the time goes:
time: 410 us; the launch traced here: 406 us
  waiting for transfers between devices  372 us (91%)
  between operations  13.8 us (3%)
  matrix products  13.2 us (3%)
    reduce_scatter x1, waiting for transfers between devices, body(): lax.psum_scatter(contract_last(pre_grad, w_in), 'section', scatter_dimens...  223 us
    reduce_scatter x1, waiting for transfers between devices, body(): lax.psum_scatter(contract_last(grad_rows, w_out), 'dp', scatter_dimension...  75.4 us
    all_gather x1, waiting for transfers between devices, body(): pre_grad = lax.all_gather(pre_grad_own, 'dp', axis=0, tiled=True)  40.1 us
    all_gather x1, waiting for transfers between devices, body(): lax.all_gather(hidden_own, 'dp', axis=0, tiled=True)  32.8 us
  transfers between devices with their start and end apart: 4, of which 4 were waited for; matrix products, arithmetic and copies ran while one was open for 3% of the time, Pallas kernels for 0%

commit v1 on v0

v1 whole, which is shorter than its diff:
```python
import math

import jax
import jax.numpy as jnp
from jax import lax
from jax.sharding import Mesh
from jax.sharding import PartitionSpec as P

inv_root_two = 1.0 / math.sqrt(2.0)
inv_root_tau = 1.0 / math.sqrt(2.0 * math.pi)

SECTION = ("y", "zh")
DP = ("x", "zl", "core")


def contract_last(left, right):
    return lax.dot_general(
        left, right, (((1,), (1,)), ((), ())), preferred_element_type=jnp.float32
    )


def contract_first(left, right):
    return lax.dot_general(
        left, right, (((0,), (0,)), ((), ())), preferred_element_type=jnp.float32
    )


def exchange_sum(part, axis, count):
    blocks = lax.all_to_all(part.astype(jnp.bfloat16), axis, 0, 0, tiled=True)
    rows = part.shape[0] // count
    return jnp.sum(blocks.reshape(count, rows, part.shape[1]).astype(jnp.float32), axis=0)


def body(inputs, out_grad, saved_codes, row_scale, w_in, w_out):
    pre_act = saved_codes.astype(jnp.float32) * row_scale[:, None]
    normal_cdf = 0.5 * (1.0 + jax.scipy.special.erf(pre_act * inv_root_two))
    hidden_own = (pre_act * normal_cdf).astype(jnp.bfloat16)
    slope_own = (normal_cdf + pre_act * jnp.exp(-0.5 * pre_act * pre_act) * inv_root_tau).astype(
        jnp.bfloat16
    )
    hidden = lax.all_gather(hidden_own, DP, axis=0, tiled=True)
    grad_share = exchange_sum(contract_last(out_grad, w_out), DP, 16)
    pre_grad_own = (grad_share * slope_own).astype(jnp.bfloat16)
    same_core = lax.all_to_all(
        jnp.tile(pre_grad_own, (8, 1)), ("x", "zl"), 0, 0, tiled=True
    )
    both = lax.all_to_all(jnp.tile(same_core, (2, 1)), "core", 0, 0, tiled=True)
    pre_grad = both.reshape(2, 8, 48, 1024).transpose(1, 0, 2, 3).reshape(768, 1024)
    input_grad = exchange_sum(contract_last(pre_grad, w_in), SECTION, 32)
    w_in_total = contract_first(inputs, pre_grad)
    w_out_total = contract_first(hidden, out_grad)
    return (
        input_grad.astype(jnp.bfloat16),
        w_in_total.astype(jnp.bfloat16),
        w_out_total.astype(jnp.bfloat16),
    )


def solution(mesh):
    cut = Mesh(mesh.devices.reshape(8, 4, 4, 2, 2), SECTION + DP)
    placed = (
        P(None, DP),
        P(None, DP),
        P(DP, SECTION),
        P(DP),
        P(DP, SECTION),
        P(SECTION, DP),
    )
    return jax.shard_map(
        body,
        mesh=cut,
        in_specs=placed,
        out_specs=(P(SECTION, DP), P(DP, SECTION), P(SECTION, DP)),
        check_vma=False,
    )
```

time: 410 us -> 118 us (0.29)
  the two profiles are of different devices: /device:TPU:1 before, /device:TPU:35 now
where the time goes in v1:
time: 118 us
  blocking collectives  33.6 us (28%)
  waiting for transfers between devices  31.5 us (27%)
  starting transfers between devices  19.5 us (17%)
  between operations  14.1 us (12%)
  matrix products  10.6 us (9%)
  local copies, waits for them, and re-layouts  6.58 us (6%)
  other arithmetic  1.82 us (2%)
    all_to_all x1, blocking collectives, exchange_sum(): blocks = lax.all_to_all(part.astype(jnp.bfloat16), axis, 0, 0, tiled=True)  26.2 us
    all_to_all x1, waiting for transfers between devices, exchange_sum(): blocks = lax.all_to_all(part.astype(jnp.bfloat16), axis, 0, 0, tiled=True)  15.3 us
    all_to_all x1, starting transfers between devices, exchange_sum(): blocks = lax.all_to_all(part.astype(jnp.bfloat16), axis, 0, 0, tiled=True)  14.4 us
    all_to_all x1, waiting for transfers between devices, body(): lax.all_to_all(jnp.tile(pre_grad_own, (8, 1)), ('x', 'zl'), 0, 0, tiled=T...  8.64 us
    all_to_all x1, blocking collectives, body(): both = lax.all_to_all(jnp.tile(same_core, (2, 1)), 'core', 0, 0, tiled=True)  7.36 us
    all_gather x1, waiting for transfers between devices, body(): hidden = lax.all_gather(hidden_own, DP, axis=0, tiled=True)  6.93 us
    dot_general x2, matrix products, contract_first(): lax.dot_general(left, right, (((0,), (0,)), ((), ())), preferred_element_...  6.53 us
    unnamed x11, local copies, waits for them, and re-layouts  5.28 us
  transfers between devices with their start and end apart: 3, of which 3 were waited for; matrix products, arithmetic and copies ran while one was open for 7% of the time, Pallas kernels for 0%

profile of v1, /device:TPU:35, one launch (start us, length us, event | category | flops | bytes accessed | tf_op | source)
XLA Modules:
  0.0 117.7 jit_solution(6844677001455680036)
XLA Ops:
  7.2 0.0 copy-start
  7.2 1.2 %copy-done = bf16[1024,512]{1,0:T(8,128)(2,1)S(1)} copy-done((bf16[1024,512]{1,0:T(8,128)(2,1)S(1)}, bf16[1024,512]{1,0:T(8,128)(2,1)}, u32[]{:S(2)}) %copy-start) | copy-done | bytes 1048600
  8.4 2.1 %convolution_convert_fusion = bf16[768,1024]{1,0:T(8,128)(2,1)S(1)} fusion(bf16[768,512]{1,0:T(8,128)(2,1)} %param.7, bf16[1024,512]{1,0:T(8,128)(2,1)S(1)} %copy-done), kind=kOutput, calls=%fused_computation.1 | convolution fusion | flops 806092800 | bytes 3407872 | tf_op jit(solution)/shard_map/dot_general | solution.py:17
  10.5 26.2 %all_to_all.30 = bf16[16,48,1024]{2,1,0:T(8,128)(2,1)S(1)} all-to-all(bf16[16,48,1024]{2,1,0:T(8,128)(2,1)S(1)} %bitcast.21), channel_id=1, replica_groups=mesh['y'=8,'zh'=4,'x'=4,'zl'=2,'core'=2] {'x','zl','core'}, dimensions={0} | all-to-all | bytes 3145728 | tf_op jit(solution)/shard_map/all_to_all | solution.py:29
  36.8 0.3 convert_reduce_fusion
  37.1 0.6 copy-done.1
  37.7 0.0 copy-done.2
  37.7 0.8 multiply_convert_fusion
  38.5 1.0 tile.6
  39.5 5.1 %all-to-all-start.1 = ((bf16[8,48,1024]{2,1,0:T(8,128)(2,1)}), bf16[8,48,1024]{2,1,0:T(8,128)(2,1)S(1)}, u32[]{:S(2)}, u32[]{:S(2)}) async-start(bf16[8,48,1024]{2,1,0:T(8,128)(2,1)} %tile.6), calls=%async_computation.1 | async-start | bytes 1572864 | tf_op jit(solution)/shard_map/all_to_all | solution.py:44
  44.6 0.7 all-gather.2.cloned.1.call-update
  45.3 8.6 %all-to-all-done.1 = bf16[8,48,1024]{2,1,0:T(8,128)(2,1)S(1)} async-done(((bf16[8,48,1024]{2,1,0:T(8,128)(2,1)}), bf16[8,48,1024]{2,1,0:T(8,128)(2,1)S(1)}, u32[]{:S(2)}, u32[]{:S(2)}) %all-to-all-start.1) | async-done | bytes 786464 | tf_op jit(solution)/shard_map/all_to_all | solution.py:44
  53.9 0.2 tile.8
  54.1 7.4 %all_to_all.31 = bf16[2,384,1024]{2,1,0:T(8,128)(2,1)S(1)} all-to-all(bf16[2,384,1024]{2,1,0:T(8,128)(2,1)S(1)} %tile.8), channel_id=1, replica_groups=mesh['y'=8,'zh'=4,'x'=4,'zl'=2,'core'=2] {'core'}, dimensions={0} | all-to-all | bytes 3145728 | tf_op jit(solution)/shard_map/all_to_all | solution.py:47
  61.5 0.1 copy.11
  61.6 1.1 copy-done.3
  62.7 1.9 %convolution_convert_fusion.3 = bf16[768,512]{1,0:T(8,128)(2,1)} fusion(bf16[768,1024]{1,0:T(8,128)(2,1)S(1)} %bitcast.19, bf16[512,1024]{1,0:T(8,128)(2,1)S(1)} %copy-done.3), kind=kOutput, calls=%fused_computation.4 | convolution fusion | flops 805699584 | bytes 3407872 | tf_op jit(solution)/shard_map/dot_general | solution.py:17
  64.6 14.4 %all-to-all-start.3 = ((bf16[32,24,512]{2,1,0:T(8,128)(2,1)}), bf16[32,24,512]{2,1,0:T(8,128)(2,1)S(1)}, u32[]{:S(2)}, u32[]{:S(2)}) async-start(bf16[32,24,512]{2,1,0:T(8,128)(2,1)} %bitcast.22), calls=%async_computation.3 | async-start | bytes 1572864 | tf_op jit(solution)/shard_map/all_to_all | solution.py:29
  79.0 3.1 %fusion = bf16[512,1024]{0,1:T(8,128)(2,1)} fusion(bf16[768,1024]{1,0:T(8,128)(2,1)S(1)} %bitcast.20, bf16[768,512]{1,0:T(8,128)(2,1)} %param.6), kind=kOutput, calls=%fused_computation.5 | convolution fusion | flops 805830656 | bytes 3407872 | tf_op jit(solution)/shard_map/dot_general | solution.py:23
  82.2 2.4 %copy.12 = bf16[512,1024]{1,0:T(8,128)(2,1)} copy(bf16[512,1024]{0,1:T(8,128)(2,1)} %fusion) | data formatting | bytes 2097152
  84.5 15.3 %all-to-all-done.3 = bf16[32,24,512]{2,1,0:T(8,128)(2,1)S(1)} async-done(((bf16[32,24,512]{2,1,0:T(8,128)(2,1)}), bf16[32,24,512]{2,1,0:T(8,128)(2,1)S(1)}, u32[]{:S(2)}, u32[]{:S(2)}) %all-to-all-start.3) | async-done | bytes 786464 | tf_op jit(solution)/shard_map/all_to_all | solution.py:29
  99.8 0.7 reduce_sum.22
  100.5 6.9 %all-gather.2.cloned.1.call-done = bf16[768,1024]{1,0:T(8,128)(2,1)} async-done(((bf16[48,1024]{1,0:T(8,128)(2,1)}), bf16[768,1024]{1,0:T(8,128)(2,1)}) %all-gather.2.cloned.1.call-update) | async-done | bytes 1572880 | tf_op jit(solution)/shard_map/all_gather | solution.py:41
  107.4 3.4 %convolution_convert_fusion.1 = bf16[1024,512]{1,0:T(8,128)(2,1)} fusion(bf16[768,1024]{1,0:T(8,128)(2,1)} %all-gather.2.cloned.1.call-done, bf16[768,512]{1,0:T(8,128)(2,1)S(1)} %copy-done.4), kind=kOutput, calls=%fused_computation.2 | convolution fusion | flops 805830656 | bytes 3407872 | tf_op jit(solution)/shard_map/dot_general | solution.py:23
  (6 shorter events, 0.0 us)
Async XLA Ops:
  7.2 1.2 %copy-start = (bf16[1024,512]{1,0:T(8,128)(2,1)S(1)}, bf16[1024,512]{1,0:T(8,128)(2,1)}, u32[]{:S(2)}) copy-start(bf16[1024,512]{1,0:T(8,128)(2,1)} %param.11) | copy-start | bytes 3145732
  36.8 0.9 copy-start.1
  36.8 0.9 copy-start.2
  39.5 14.5 %all-to-all-start.1 = ((bf16[8,48,1024]{2,1,0:T(8,128)(2,1)}), bf16[8,48,1024]{2,1,0:T(8,128)(2,1)S(1)}, u32[]{:S(2)}, u32[]{:S(2)}) async-start(bf16[8,48,1024]{2,1,0:T(8,128)(2,1)} %tile.6), calls=%async_computation.1 | async-start | bytes 1572864 | tf_op jit(solution)/shard_map/all_to_all | solution.py:44
  44.6 62.8 %all-gather.2.cloned.1.call-start = ((), (), s32[]{:S(2)}) async-start(), calls=%async_computation.4 | async-start | bytes 1671168 | tf_op jit(solution)/shard_map/all_gather | solution.py:41
  61.5 1.2 %copy-start.3 = (bf16[512,1024]{1,0:T(8,128)(2,1)S(1)}, bf16[512,1024]{1,0:T(8,128)(2,1)}, u32[]{:S(2)}) copy-start(bf16[512,1024]{1,0:T(8,128)(2,1)} %param.10) | copy-start | bytes 3145732
  64.6 35.1 %all-to-all-start.3 = ((bf16[32,24,512]{2,1,0:T(8,128)(2,1)}), bf16[32,24,512]{2,1,0:T(8,128)(2,1)S(1)}, u32[]{:S(2)}, u32[]{:S(2)}) async-start(bf16[32,24,512]{2,1,0:T(8,128)(2,1)} %bitcast.22), calls=%async_computation.3 | async-start | bytes 1572864 | tf_op jit(solution)/shard_map/all_to_all | solution.py:29
  82.2 25.3 %copy-start.4 = (bf16[768,512]{1,0:T(8,128)(2,1)S(1)}, bf16[768,512]{1,0:T(8,128)(2,1)}, u32[]{:S(2)}) copy-start(bf16[768,512]{1,0:T(8,128)(2,1)} %param.7) | copy-start | bytes 2359300
Sparse Core Ops, SparseCore 0:
  47.5 59.8 all-gather.1

commit v2 on v1

--- a/solution.py
+++ b/solution.py
@@ -10,6 +10,7 @@
 inv_root_tau = 1.0 / math.sqrt(2.0 * math.pi)
 
 SECTION = ("y", "zh")
+CHIPS = ("x", "zl")
 DP = ("x", "zl", "core")
 
 
@@ -25,10 +26,27 @@
     )
 
 
-def exchange_sum(part, axis, count):
-    blocks = lax.all_to_all(part.astype(jnp.bfloat16), axis, 0, 0, tiled=True)
-    rows = part.shape[0] // count
-    return jnp.sum(blocks.reshape(count, rows, part.shape[1]).astype(jnp.float32), axis=0)
+def core_swap(block):
+    return lax.ppermute(block, "core", [(0, 1), (1, 0)])
+
+
+def split_cores(rows):
+    me = lax.axis_index("core")
+    cut = rows.reshape(8, 2, 48, rows.shape[1])
+    mine = lax.dynamic_index_in_dim(cut, me, 1, keepdims=False)
+    other = lax.dynamic_index_in_dim(cut, 1 - me, 1, keepdims=False)
+    return mine.reshape(384, -1), other.reshape(384, -1)
+
+
+def join_cores(mine, other):
+    first = lax.axis_index("core") == 0
+    mine, other = mine.reshape(8, 48, -1), other.reshape(8, 48, -1)
+    both = jnp.stack([jnp.where(first, mine, other), jnp.where(first, other, mine)], axis=1)
+    return both.reshape(768, -1)
+
+
+def copies_to_chips(block):
+    return lax.all_to_all(jnp.tile(block, (8, 1)), CHIPS, 0, 0, tiled=True)
 
 
 def body(inputs, out_grad, saved_codes, row_scale, w_in, w_out):
@@ -38,17 +56,34 @@
     slope_own = (normal_cdf + pre_act * jnp.exp(-0.5 * pre_act * pre_act) * inv_root_tau).astype(
         jnp.bfloat16
     )
-    hidden = lax.all_gather(hidden_own, DP, axis=0, tiled=True)
-    grad_share = exchange_sum(contract_last(out_grad, w_out), DP, 16)
+    hidden_own, slope_own = lax.optimization_barrier((hidden_own, slope_own))
+
+    grad_mine, grad_other = split_cores(out_grad)
+    received = core_swap(contract_last(grad_other, w_out).astype(jnp.bfloat16))
+    own_sum = lax.optimization_barrier(contract_last(grad_mine, w_out))
+    chip_sum = own_sum + received.astype(jnp.float32)
+    blocks = lax.all_to_all(chip_sum.astype(jnp.bfloat16), CHIPS, 0, 0, tiled=True)
+    hidden_pair = lax.all_gather(hidden_own, "zl", axis=0, tiled=True)
+    blocks, hidden_pair = lax.optimization_barrier((blocks, hidden_pair))
+    grad_share = jnp.sum(blocks.reshape(8, 48, 1024).astype(jnp.float32), axis=0)
     pre_grad_own = (grad_share * slope_own).astype(jnp.bfloat16)
-    same_core = lax.all_to_all(
-        jnp.tile(pre_grad_own, (8, 1)), ("x", "zl"), 0, 0, tiled=True
+
+    mine = copies_to_chips(pre_grad_own)
+    other = core_swap(mine)
+    partial = join_cores(
+        contract_last(mine, w_in).astype(jnp.bfloat16),
+        contract_last(other, w_in).astype(jnp.bfloat16),
     )
-    both = lax.all_to_all(jnp.tile(same_core, (2, 1)), "core", 0, 0, tiled=True)
-    pre_grad = both.reshape(2, 8, 48, 1024).transpose(1, 0, 2, 3).reshape(768, 1024)
-    input_grad = exchange_sum(contract_last(pre_grad, w_in), SECTION, 32)
-    w_in_total = contract_first(inputs, pre_grad)
-    w_out_total = contract_first(hidden, out_grad)
+    hidden_pair, partial = lax.optimization_barrier((hidden_pair, partial))
+    blocks = lax.all_to_all(partial, SECTION, 0, 0, tiled=True)
+    input_grad = jnp.sum(blocks.reshape(32, 24, 512).astype(jnp.float32), axis=0)
+
+    hidden_mine = lax.all_gather(hidden_pair, "x", axis=0, tiled=True)
+    hidden_mine, mine, other, inputs = lax.optimization_barrier((hidden_mine, mine, other, inputs))
+    hidden_other = core_swap(hidden_mine)
+    inputs_mine, inputs_other = split_cores(inputs)
+    w_in_total = contract_first(inputs_mine, mine) + contract_first(inputs_other, other)
+    w_out_total = contract_first(hidden_mine, grad_mine) + contract_first(hidden_other, grad_other)
     return (
         input_grad.astype(jnp.bfloat16),
         w_in_total.astype(jnp.bfloat16),

time: 118 us -> 90.6 us (0.77)
  the two profiles are of different devices: /device:TPU:35 before, /device:TPU:1 now
where the time goes in v2:
time: 90.6 us; the launch traced here: 89.2 us
  blocking collectives  39.4 us (43%)
  starting transfers between devices  33.2 us (37%)
  matrix products  8.67 us (10%)
  other arithmetic  3.13 us (3%)
  local copies, waits for them, and re-layouts  2.74 us (3%)
  waiting for transfers between devices  1.27 us (1%)
    ppermute x3, starting transfers between devices, core_swap(): return lax.ppermute(block, 'core', [(0, 1), (1, 0)])  18.3 us
    all_to_all x1, blocking collectives, copies_to_chips(): return lax.all_to_all(jnp.tile(block, (8, 1)), CHIPS, 0, 0, tiled=True)  15.3 us
    all_gather x1, blocking collectives, body(): hidden_pair = lax.all_gather(hidden_own, 'zl', axis=0, tiled=True)  12.5 us
    all_gather x1, blocking collectives, body(): hidden_mine = lax.all_gather(hidden_pair, 'x', axis=0, tiled=True)  11.7 us
    all_to_all x1, starting transfers between devices, body(): blocks = lax.all_to_all(partial, SECTION, 0, 0, tiled=True)  11.3 us
    dot_general x4, matrix products, contract_first(): lax.dot_general(left, right, (((0,), (0,)), ((), ())), preferred_element_...  4.96 us
    dot_general x4, matrix products, contract_last(): lax.dot_general(left, right, (((1,), (1,)), ((), ())), preferred_element_...  3.72 us
    all_to_all x1, starting transfers between devices, body(): lax.all_to_all(chip_sum.astype(jnp.bfloat16), CHIPS, 0, 0, tiled=True)  3.55 us
  transfers between devices with their start and end apart: 5, of which 1 were waited for; matrix products, arithmetic and copies ran while one was open for 10% of the time, Pallas kernels for 0%

profile of v2, /device:TPU:1, one launch (start us, length us, event | category | flops | bytes accessed | tf_op | source)
XLA Modules:
  0.0 89.2 jit_solution(14693494006573259571)
XLA Ops:
  0.7 1.3 %constant_dynamic-slice_fusion.2 = (bf16[8,1,48,512]{3,2,1,0:T(8,128)(2,1)S(1)}, bf16[8,1,48,512]{3,2,1,0:T(8,128)(2,1)S(1)}) fusion(bf16[8,2,48,512]{3,2,1,0:T(8,128)(2,1)} %bitcast.44, s32[]{:T(128)S(6)} %select_n.42, s32[]{:T(128)S(6)} %select_n.41), kind=kLoop, calls=%fused_computation.22 | loop fusion | bytes 1572872 | tf_op jit(solution)/shard_map/jit(dynamic_index_in_dim)/dynamic_slice | solution.py:37
  1.9 0.2 copy-done
  2.1 0.6 convolution_convert_fusion
  2.7 8.8 %collective-permute-start = (bf16[384,1024]{1,0:T(8,128)(2,1)S(1)}, bf16[384,1024]{1,0:T(8,128)(2,1)S(1)}, u32[]{:S(2)}, u32[]{:S(2)}) collective-permute-start(bf16[384,1024]{1,0:T(8,128)(2,1)S(1)} %convolution_convert_fusion), channel_id=1, source_target_pairs={{0,1},{1,0},{2,3},{3,2},{4,5},{5,4},{6,7},{7,6},{8,9},{9,8},{10,11... | collective-permute-start | bytes 2359304 | tf_op jit(solution)/shard_map/ppermute | solution.py:30
  11.5 0.6 fusion.5
  12.1 1.3 %collective-permute-done = bf16[384,1024]{1,0:T(8,128)(2,1)S(1)} collective-permute-done((bf16[384,1024]{1,0:T(8,128)(2,1)S(1)}, bf16[384,1024]{1,0:T(8,128)(2,1)S(1)}, u32[]{:S(2)}, u32[]{:S(2)}) %collective-permute-start) | collective-permute-done | bytes 786464 | tf_op jit(solution)/shard_map/ppermute | solution.py:30
  13.4 1.1 %add_convert_fusion.2 = bf16[384,1024]{1,0:T(8,128)(2,1)} fusion(f32[384,1024]{1,0:T(8,128)S(1)} %fusion.5, bf16[384,1024]{1,0:T(8,128)(2,1)S(1)} %collective-permute-done), kind=kLoop, calls=%fused_computation.3 | loop fusion | flops 1179648 | bytes 3145728 | tf_op jit(solution)/shard_map/convert_element_type | solution.py:65
  14.5 3.5 %all-to-all-start = ((bf16[8,48,1024]{2,1,0:T(8,128)(2,1)}), bf16[8,48,1024]{2,1,0:T(8,128)(2,1)S(1)}, u32[]{:S(2)}, u32[]{:S(2)}) async-start(bf16[8,48,1024]{2,1,0:T(8,128)(2,1)} %bitcast.3), calls=%async_computation | async-start | bytes 1572864 | tf_op jit(solution)/shard_map/all_to_all | solution.py:65
  18.1 0.2 fusion.4
  18.3 12.5 %all_gather.6 = bf16[96,1024]{1,0:T(8,128)(2,1)} all-gather(bf16[48,1024]{1,0:T(8,128)(2,1)S(1)} %get-tuple-element.13), channel_id=1, replica_groups=mesh['y'=8,'zh'=4,'x'=4,'zl'=2,'core'=2] {'zl'}, dimensions={0}, use_global_device_ids=true | all-gather | bytes 294912 | tf_op jit(solution)/shard_map/all_gather | solution.py:66
  31.0 15.3 %all_to_all.30 = bf16[8,48,1024]{2,1,0:T(8,128)(2,1)S(1)} all-to-all(bf16[8,48,1024]{2,1,0:T(8,128)(2,1)S(1)} %tile.2), channel_id=1, replica_groups=mesh['y'=8,'zh'=4,'x'=4,'zl'=2,'core'=2] {'x','zl'}, dimensions={0} | all-to-all | bytes 1572864 | tf_op jit(solution)/shard_map/all_to_all | solution.py:49
  46.2 4.3 %collective-permute-start.1 = (bf16[384,1024]{1,0:T(8,128)(2,1)S(1)}, bf16[384,1024]{1,0:T(8,128)(2,1)S(1)}, u32[]{:S(2)}, u32[]{:S(2)}) collective-permute-start(bf16[384,1024]{1,0:T(8,128)(2,1)S(1)} %bitcast.37), channel_id=1, source_target_pairs={{0,1},{1,0},{2,3},{3,2},{4,5},{5,4},{6,7},{7,6},{8,9},{9,8},{10,11... | collective-permute-start | bytes 2359304 | tf_op jit(solution)/shard_map/ppermute | solution.py:30
  50.6 1.9 %convolution_convert_fusion.2 = bf16[384,512]{1,0:T(8,128)(2,1)S(1)} fusion(bf16[384,1024]{1,0:T(8,128)(2,1)S(1)} %bitcast.38, bf16[512,1024]{1,0:T(8,128)(2,1)} %param.10), kind=kOutput, calls=%fused_computation.6 | convolution fusion | flops 402849792 | bytes 2228224 | tf_op jit(solution)/shard_map/dot_general | solution.py:18
  52.5 0.6 broadcast_select_fusion.1
  53.1 1.0 %pad_maximum_fusion = bf16[8,2,48,512]{3,2,1,0:T(8,128)(2,1)} fusion(bf16[8,1,48,512]{3,2,1,0:T(8,128)(2,1)S(1)} %bitcast.47, bf16[8,1,48,512]{3,2,1,0:T(8,128)(2,1)S(1)} %bitcast.46), kind=kLoop, calls=%fused_computation.7 | loop fusion | flops 393216 | bytes 1572864 | tf_op jit(solution)/shard_map/stack | solution.py:44
  54.1 11.3 %all-to-all-start.2 = ((bf16[32,24,512]{2,1,0:T(8,128)(2,1)}), bf16[32,24,512]{2,1,0:T(8,128)(2,1)S(1)}, u32[]{:S(2)}, u32[]{:S(2)}) async-start(bf16[32,24,512]{2,1,0:T(8,128)(2,1)} %bitcast.12), calls=%async_computation.2 | async-start | bytes 1572864 | tf_op jit(solution)/shard_map/all_to_all | solution.py:78
  65.4 11.7 %all_gather.7 = bf16[384,1024]{1,0:T(8,128)(2,1)S(1)} all-gather(bf16[96,1024]{1,0:T(8,128)(2,1)} %all_gather.6), channel_id=1, replica_groups=mesh['y'=8,'zh'=4,'x'=4,'zl'=2,'core'=2] {'x'}, dimensions={0}, use_global_device_ids=true | all-gather | bytes 983040 | tf_op jit(solution)/shard_map/all_gather | solution.py:81
  77.1 5.2 %collective-permute-start.2 = (bf16[384,1024]{1,0:T(8,128)(2,1)S(1)}, bf16[384,1024]{1,0:T(8,128)(2,1)S(1)}, u32[]{:S(2)}, u32[]{:S(2)}) collective-permute-start(bf16[384,1024]{1,0:T(8,128)(2,1)S(1)} %all_gather.7), channel_id=1, source_target_pairs={{0,1},{1,0},{2,3},{3,2},{4,5},{5,4},{6,7},{7,6},{8,9},{9,8},{10,11... | collective-permute-start | bytes 2359304 | tf_op jit(solution)/shard_map/ppermute | solution.py:30
  82.3 1.2 %constant_dynamic-slice_fusion.1 = (bf16[8,1,48,512]{3,2,1,0:T(8,128)(2,1)S(1)}, bf16[8,1,48,512]{3,2,1,0:T(8,128)(2,1)S(1)}) fusion(bf16[8,2,48,512]{3,2,1,0:T(8,128)(2,1)} %bitcast.45, s32[]{:T(128)S(6)} %select_n.41, s32[]{:T(128)S(6)} %select_n.42), kind=kLoop, calls=%fused_computation.21 | loop fusion | bytes 1572872 | tf_op jit(solution)/shard_map/jit(dynamic_index_in_dim)/dynamic_slice | solution.py:36
  83.5 0.7 fusion.6
  84.3 1.7 %add_convert_fusion.1 = bf16[512,1024]{1,0:T(8,128)(2,1)} fusion(f32[512,1024]{1,0:T(8,128)S(1)} %fusion.6, bf16[384,512]{1,0:T(8,128)(2,1)S(1)} %bitcast.42, bf16[384,1024]{1,0:T(8,128)(2,1)S(1)} %bitcast.39), kind=kOutput, calls=%fused_computation.1 | convolution fusion | flops 403701760 | bytes 4325376 | tf_op jit(solution)/shard_map/dot_general | solution.py:24
  86.0 0.8 fusion.7
  86.7 1.8 %add_convert_fusion = bf16[1024,512]{1,0:T(8,128)(2,1)} fusion(f32[1024,512]{1,0:T(8,128)S(1)} %fusion.7, bf16[384,1024]{1,0:T(8,128)(2,1)S(1)} %all_gather.7, bf16[384,512]{1,0:T(8,128)(2,1)S(1)} %bitcast.36), kind=kOutput, calls=%fused_computation | convolution fusion | flops 403701760 | bytes 4325376 | tf_op jit(solution)/shard_map/dot_general | solution.py:24
  88.5 0.7 reduce_sum.22
  (18 shorter events, 0.3 us)
Async XLA Ops:
  0.6 1.5 %copy-start = (bf16[1024,512]{1,0:T(8,128)(2,1)S(1)}, bf16[1024,512]{1,0:T(8,128)(2,1)}, u32[]{:S(2)}) copy-start(bf16[1024,512]{1,0:T(8,128)(2,1)} %param.11) | copy-start | bytes 3145732
  2.7 10.7 %collective-permute-start = (bf16[384,1024]{1,0:T(8,128)(2,1)S(1)}, bf16[384,1024]{1,0:T(8,128)(2,1)S(1)}, u32[]{:S(2)}, u32[]{:S(2)}) collective-permute-start(bf16[384,1024]{1,0:T(8,128)(2,1)S(1)} %convolution_convert_fusion), channel_id=1, source_target_pairs={{0,1},{1,0},{2,3},{3,2},{4,5},{5,4},{6,7},{7,6},{8,9},{9,8},{10,11... | collective-permute-start | bytes 2359304 | tf_op jit(solution)/shard_map/ppermute | solution.py:30
  12.1 6.0 %copy-start.3 = (s32[48,1024]{1,0:T(8,128)S(1)}, s32[48,1024]{1,0:T(8,128)}, u32[]{:S(2)}) copy-start(s32[48,1024]{1,0:T(8,128)} %param.8) | copy-start | bytes 589828
  12.1 6.0 %copy-start.4 = (f32[48]{0:T(128)S(1)}, f32[48]{0:T(128)}, u32[]{:S(2)}) copy-start(f32[48]{0:T(128)} %param.9) | copy-start | bytes 580
  14.5 16.2 %all-to-all-start = ((bf16[8,48,1024]{2,1,0:T(8,128)(2,1)}), bf16[8,48,1024]{2,1,0:T(8,128)(2,1)S(1)}, u32[]{:S(2)}, u32[]{:S(2)}) async-start(bf16[8,48,1024]{2,1,0:T(8,128)(2,1)} %bitcast.3), calls=%async_computation | async-start | bytes 1572864 | tf_op jit(solution)/shard_map/all_to_all | solution.py:65
  46.2 6.2 %collective-permute-start.1 = (bf16[384,1024]{1,0:T(8,128)(2,1)S(1)}, bf16[384,1024]{1,0:T(8,128)(2,1)S(1)}, u32[]{:S(2)}, u32[]{:S(2)}) collective-permute-start(bf16[384,1024]{1,0:T(8,128)(2,1)S(1)} %bitcast.37), channel_id=1, source_target_pairs={{0,1},{1,0},{2,3},{3,2},{4,5},{5,4},{6,7},{7,6},{8,9},{9,8},{10,11... | collective-permute-start | bytes 2359304 | tf_op jit(solution)/shard_map/ppermute | solution.py:30
  50.6 1.9 %copy-start.5 = (bf16[512,1024]{1,0:T(8,128)(2,1)S(1)}, bf16[512,1024]{1,0:T(8,128)(2,1)}, u32[]{:S(2)}) copy-start(bf16[512,1024]{1,0:T(8,128)(2,1)} %param.10) | copy-start | bytes 3145732
  52.5 1.6 %copy-start.1 = (bf16[384,1024]{1,0:T(8,128)(2,1)}, bf16[384,1024]{1,0:T(8,128)(2,1)S(1)}, u32[]{:S(2)}) copy-start(bf16[384,1024]{1,0:T(8,128)(2,1)S(1)} %collective-permute-done.1) | copy-start | bytes 2359300
  54.1 34.4 %all-to-all-start.2 = ((bf16[32,24,512]{2,1,0:T(8,128)(2,1)}), bf16[32,24,512]{2,1,0:T(8,128)(2,1)S(1)}, u32[]{:S(2)}, u32[]{:S(2)}) async-start(bf16[32,24,512]{2,1,0:T(8,128)(2,1)} %bitcast.12), calls=%async_computation.2 | async-start | bytes 1572864 | tf_op jit(solution)/shard_map/all_to_all | solution.py:78
  65.4 18.1 %copy-start.2 = (bf16[384,1024]{1,0:T(8,128)(2,1)S(1)}, bf16[384,1024]{1,0:T(8,128)(2,1)}, u32[]{:S(2)}) copy-start(bf16[384,1024]{1,0:T(8,128)(2,1)} %copy-done.1) | copy-start | bytes 2359300
  77.1 8.9 %collective-permute-start.2 = (bf16[384,1024]{1,0:T(8,128)(2,1)S(1)}, bf16[384,1024]{1,0:T(8,128)(2,1)S(1)}, u32[]{:S(2)}, u32[]{:S(2)}) collective-permute-start(bf16[384,1024]{1,0:T(8,128)(2,1)S(1)} %all_gather.7), channel_id=1, source_target_pairs={{0,1},{1,0},{2,3},{3,2},{4,5},{5,4},{6,7},{7,6},{8,9},{9,8},{10,11... | collective-permute-start | bytes 2359304 | tf_op jit(solution)/shard_map/ppermute | solution.py:30

commit v3 on v2

--- a/solution.py
+++ b/solution.py
@@ -60,8 +60,13 @@
 
     grad_mine, grad_other = split_cores(out_grad)
     received = core_swap(contract_last(grad_other, w_out).astype(jnp.bfloat16))
-    own_sum = lax.optimization_barrier(contract_last(grad_mine, w_out))
-    chip_sum = own_sum + received.astype(jnp.float32)
+    own_sum = lax.optimization_barrier(contract_last(grad_mine, w_out).astype(jnp.bfloat16))
+    inputs, grad_mine = lax.optimization_barrier((inputs, grad_mine))
+    inputs_mine, inputs_other = split_cores(inputs)
+    received, inputs_mine, inputs_other = lax.optimization_barrier(
+        (received, inputs_mine, inputs_other)
+    )
+    chip_sum = own_sum.astype(jnp.float32) + received.astype(jnp.float32)
     blocks = lax.all_to_all(chip_sum.astype(jnp.bfloat16), CHIPS, 0, 0, tiled=True)
     hidden_pair = lax.all_gather(hidden_own, "zl", axis=0, tiled=True)
     blocks, hidden_pair = lax.optimization_barrier((blocks, hidden_pair))
@@ -79,9 +84,7 @@
     input_grad = jnp.sum(blocks.reshape(32, 24, 512).astype(jnp.float32), axis=0)
 
     hidden_mine = lax.all_gather(hidden_pair, "x", axis=0, tiled=True)
-    hidden_mine, mine, other, inputs = lax.optimization_barrier((hidden_mine, mine, other, inputs))
     hidden_other = core_swap(hidden_mine)
-    inputs_mine, inputs_other = split_cores(inputs)
     w_in_total = contract_first(inputs_mine, mine) + contract_first(inputs_other, other)
     w_out_total = contract_first(hidden_mine, grad_mine) + contract_first(hidden_other, grad_other)
     return (

time: 90.6 us -> 90.6 us (level)
    ppermute x3, waiting for transfers between devices: 1.26 us -> 0.32 us  [core_swap(): return lax.ppermute(block, 'core', [(0, 1), (1, 0)])]
  transfers between devices with their start and end apart: 5 -> 5, of which waited for: 1 -> 2; matrix products, arithmetic and copies ran while one was open for 10% -> 10% of each run, Pallas kernels for 0% -> 0%
where the time goes in v3:
time: 90.6 us; the launch traced here: 88.8 us
  blocking collectives  39.4 us (43%)
  starting transfers between devices  33.2 us (37%)
  matrix products  8.64 us (10%)
  other arithmetic  3.2 us (4%)
  local copies, waits for them, and re-layouts  2.78 us (3%)
    ppermute x3, starting transfers between devices, core_swap(): return lax.ppermute(block, 'core', [(0, 1), (1, 0)])  18.3 us
    all_to_all x1, blocking collectives, copies_to_chips(): return lax.all_to_all(jnp.tile(block, (8, 1)), CHIPS, 0, 0, tiled=True)  15.3 us
    all_gather x1, blocking collectives, body(): hidden_pair = lax.all_gather(hidden_own, 'zl', axis=0, tiled=True)  12.5 us
    all_gather x1, blocking collectives, body(): hidden_mine = lax.all_gather(hidden_pair, 'x', axis=0, tiled=True)  11.7 us
    all_to_all x1, starting transfers between devices, body(): blocks = lax.all_to_all(partial, SECTION, 0, 0, tiled=True)  11.3 us
    dot_general x4, matrix products, contract_first(): lax.dot_general(left, right, (((0,), (0,)), ((), ())), preferred_element_...  4.91 us
    dot_general x4, matrix products, contract_last(): lax.dot_general(left, right, (((1,), (1,)), ((), ())), preferred_element_...  3.73 us
    all_to_all x1, starting transfers between devices, body(): lax.all_to_all(chip_sum.astype(jnp.bfloat16), CHIPS, 0, 0, tiled=True)  3.55 us
  transfers between devices with their start and end apart: 5, of which 2 were waited for; matrix products, arithmetic and copies ran while one was open for 10% of the time, Pallas kernels for 0%

profile of v3, /device:TPU:1, one launch (start us, length us, event | category | flops | bytes accessed | tf_op | source)
XLA Modules:
  0.0 88.8 jit_solution(11899157297858861428)
XLA Ops:
  0.7 1.3 %constant_dynamic-slice_fusion.3 = (bf16[8,1,48,512]{3,2,1,0:T(8,128)(2,1)S(1)}, bf16[8,1,48,512]{3,2,1,0:T(8,128)(2,1)S(1)}) fusion(bf16[8,2,48,512]{3,2,1,0:T(8,128)(2,1)} %bitcast.44, s32[]{:T(128)S(6)} %select_n.41, s32[]{:T(128)S(6)} %select_n.42), kind=kLoop, calls=%fused_computation.24 | loop fusion | bytes 1572872 | tf_op jit(solution)/shard_map/jit(dynamic_index_in_dim)/dynamic_slice | solution.py:36
  2.1 0.6 convolution_convert_fusion
  2.7 8.8 %collective-permute-start = (bf16[384,1024]{1,0:T(8,128)(2,1)S(1)}, bf16[384,1024]{1,0:T(8,128)(2,1)S(1)}, u32[]{:S(2)}, u32[]{:S(2)}) collective-permute-start(bf16[384,1024]{1,0:T(8,128)(2,1)S(1)} %convolution_convert_fusion), channel_id=1, source_target_pairs={{0,1},{1,0},{2,3},{3,2},{4,5},{5,4},{6,7},{7,6},{8,9},{9,8},{10,11... | collective-permute-start | bytes 2359304 | tf_op jit(solution)/shard_map/ppermute | solution.py:30
  11.5 0.6 convolution_convert_fusion.1
  12.1 1.0 %constant_dynamic-slice_fusion = (bf16[8,1,48,512]{3,2,1,0:T(8,128)(2,1)}, bf16[8,1,48,512]{3,2,1,0:T(8,128)(2,1)}) fusion(bf16[8,2,48,512]{3,2,1,0:T(8,128)(2,1)S(1)} %bitcast.45, s32[]{:T(128)S(6)} %select_n.42, s32[]{:T(128)S(6)} %select_n.41), kind=kLoop, calls=%fused_computation.21 | loop fusion | bytes 1572872 | tf_op jit(solution)/shard_map/jit(dynamic_index_in_dim)/dynamic_slice | solution.py:37
  13.1 0.3 collective-permute-done
  13.4 1.2 %add_convert_fusion.2 = bf16[384,1024]{1,0:T(8,128)(2,1)} fusion(bf16[384,1024]{1,0:T(8,128)(2,1)S(1)} %collective-permute-done, bf16[384,1024]{1,0:T(8,128)(2,1)S(1)} %convolution_convert_fusion.1), kind=kLoop, calls=%fused_computation.3 | loop fusion | flops 1572864 | bytes 2359296 | tf_op jit(solution)/shard_map/convert_element_type | solution.py:70
  14.6 3.5 %all-to-all-start = ((bf16[8,48,1024]{2,1,0:T(8,128)(2,1)}), bf16[8,48,1024]{2,1,0:T(8,128)(2,1)S(1)}, u32[]{:S(2)}, u32[]{:S(2)}) async-start(bf16[8,48,1024]{2,1,0:T(8,128)(2,1)} %bitcast.6), calls=%async_computation | async-start | bytes 1572864 | tf_op jit(solution)/shard_map/all_to_all | solution.py:70
  18.3 12.5 %all_gather.6 = bf16[96,1024]{1,0:T(8,128)(2,1)} all-gather(bf16[48,1024]{1,0:T(8,128)(2,1)S(1)} %get-tuple-element.16), channel_id=1, replica_groups=mesh['y'=8,'zh'=4,'x'=4,'zl'=2,'core'=2] {'zl'}, dimensions={0}, use_global_device_ids=true | all-gather | bytes 294912 | tf_op jit(solution)/shard_map/all_gather | solution.py:71
  31.0 15.3 %all_to_all.30 = bf16[8,48,1024]{2,1,0:T(8,128)(2,1)S(1)} all-to-all(bf16[8,48,1024]{2,1,0:T(8,128)(2,1)S(1)} %tile.2), channel_id=1, replica_groups=mesh['y'=8,'zh'=4,'x'=4,'zl'=2,'core'=2] {'x','zl'}, dimensions={0} | all-to-all | bytes 1572864 | tf_op jit(solution)/shard_map/all_to_all | solution.py:49
  46.3 4.3 %collective-permute-start.1 = (bf16[384,1024]{1,0:T(8,128)(2,1)S(1)}, bf16[384,1024]{1,0:T(8,128)(2,1)S(1)}, u32[]{:S(2)}, u32[]{:S(2)}) collective-permute-start(bf16[384,1024]{1,0:T(8,128)(2,1)S(1)} %bitcast.35), channel_id=1, source_target_pairs={{0,1},{1,0},{2,3},{3,2},{4,5},{5,4},{6,7},{7,6},{8,9},{9,8},{10,11... | collective-permute-start | bytes 2359304 | tf_op jit(solution)/shard_map/ppermute | solution.py:30
  50.6 1.9 %convolution_convert_fusion.3 = bf16[384,512]{1,0:T(8,128)(2,1)S(1)} fusion(bf16[384,1024]{1,0:T(8,128)(2,1)S(1)} %bitcast.36, bf16[512,1024]{1,0:T(8,128)(2,1)} %param.10), kind=kOutput, calls=%fused_computation.7 | convolution fusion | flops 402849792 | bytes 2228224 | tf_op jit(solution)/shard_map/dot_general | solution.py:18
  52.6 0.6 broadcast_select_fusion.1
  53.2 1.0 %pad_maximum_fusion = bf16[8,2,48,512]{3,2,1,0:T(8,128)(2,1)} fusion(bf16[8,1,48,512]{3,2,1,0:T(8,128)(2,1)S(1)} %bitcast.47, bf16[8,1,48,512]{3,2,1,0:T(8,128)(2,1)S(1)} %bitcast.46), kind=kLoop, calls=%fused_computation.8 | loop fusion | flops 393216 | bytes 1572864 | tf_op jit(solution)/shard_map/stack | solution.py:44
  54.2 11.3 %all-to-all-start.2 = ((bf16[32,24,512]{2,1,0:T(8,128)(2,1)}), bf16[32,24,512]{2,1,0:T(8,128)(2,1)S(1)}, u32[]{:S(2)}, u32[]{:S(2)}) async-start(bf16[32,24,512]{2,1,0:T(8,128)(2,1)} %bitcast.15), calls=%async_computation.2 | async-start | bytes 1572864 | tf_op jit(solution)/shard_map/all_to_all | solution.py:83
  65.5 11.7 %all_gather.7 = bf16[384,1024]{1,0:T(8,128)(2,1)S(1)} all-gather(bf16[96,1024]{1,0:T(8,128)(2,1)} %all_gather.6), channel_id=1, replica_groups=mesh['y'=8,'zh'=4,'x'=4,'zl'=2,'core'=2] {'x'}, dimensions={0}, use_global_device_ids=true | all-gather | bytes 983040 | tf_op jit(solution)/shard_map/all_gather | solution.py:86
  77.2 5.2 %collective-permute-start.2 = (bf16[384,1024]{1,0:T(8,128)(2,1)S(1)}, bf16[384,1024]{1,0:T(8,128)(2,1)S(1)}, u32[]{:S(2)}, u32[]{:S(2)}) collective-permute-start(bf16[384,1024]{1,0:T(8,128)(2,1)S(1)} %all_gather.7), channel_id=1, source_target_pairs={{0,1},{1,0},{2,3},{3,2},{4,5},{5,4},{6,7},{7,6},{8,9},{9,8},{10,11... | collective-permute-start | bytes 2359304 | tf_op jit(solution)/shard_map/ppermute | solution.py:30
  82.4 0.8 fusion.6
  83.2 0.7 fusion.5
  83.9 0.3 copy-done.1
  84.2 1.7 %add_convert_fusion.1 = bf16[512,1024]{1,0:T(8,128)(2,1)} fusion(f32[512,1024]{1,0:T(8,128)S(1)} %fusion.5, bf16[384,512]{1,0:T(8,128)(2,1)S(1)} %bitcast.42, bf16[384,1024]{1,0:T(8,128)(2,1)S(1)} %bitcast.37), kind=kOutput, calls=%fused_computation.1 | convolution fusion | flops 403701760 | bytes 4325376 | tf_op jit(solution)/shard_map/dot_general | solution.py:24
  85.9 1.7 %add_convert_fusion = bf16[1024,512]{1,0:T(8,128)(2,1)} fusion(f32[1024,512]{1,0:T(8,128)S(1)} %fusion.6, bf16[384,1024]{1,0:T(8,128)(2,1)S(1)} %collective-permute-done.2, bf16[384,512]{1,0:T(8,128)(2,1)S(1)} %bitcast.39), kind=kOutput, calls=%fused_computation | convolution fusion | flops 403701760 | bytes 4325376 | tf_op jit(solution)/shard_map/dot_general | solution.py:24
  87.6 0.5 all-to-all-done.2
  88.1 0.7 reduce_sum.22
  (24 shorter events, 0.6 us)
Async XLA Ops:
  0.6 1.5 %copy-start = (bf16[1024,512]{1,0:T(8,128)(2,1)S(1)}, bf16[1024,512]{1,0:T(8,128)(2,1)}, u32[]{:S(2)}) copy-start(bf16[1024,512]{1,0:T(8,128)(2,1)} %param.11) | copy-start | bytes 3145732
  2.1 10.0 %copy-start.3 = (bf16[768,512]{1,0:T(8,128)(2,1)S(1)}, bf16[768,512]{1,0:T(8,128)(2,1)}, u32[]{:S(2)}) copy-start(bf16[768,512]{1,0:T(8,128)(2,1)} %param.6) | copy-start | bytes 2359300
  2.7 10.7 %collective-permute-start = (bf16[384,1024]{1,0:T(8,128)(2,1)S(1)}, bf16[384,1024]{1,0:T(8,128)(2,1)S(1)}, u32[]{:S(2)}, u32[]{:S(2)}) collective-permute-start(bf16[384,1024]{1,0:T(8,128)(2,1)S(1)} %convolution_convert_fusion), channel_id=1, source_target_pairs={{0,1},{1,0},{2,3},{3,2},{4,5},{5,4},{6,7},{7,6},{8,9},{9,8},{10,11... | collective-permute-start | bytes 2359304 | tf_op jit(solution)/shard_map/ppermute | solution.py:30
  13.1 5.1 %copy-start.6 = (s32[48,1024]{1,0:T(8,128)S(1)}, s32[48,1024]{1,0:T(8,128)}, u32[]{:S(2)}) copy-start(s32[48,1024]{1,0:T(8,128)} %param.8) | copy-start | bytes 589828
  13.1 5.1 %copy-start.7 = (f32[48]{0:T(128)S(1)}, f32[48]{0:T(128)}, u32[]{:S(2)}) copy-start(f32[48]{0:T(128)} %param.9) | copy-start | bytes 580
  14.6 16.2 %all-to-all-start = ((bf16[8,48,1024]{2,1,0:T(8,128)(2,1)}), bf16[8,48,1024]{2,1,0:T(8,128)(2,1)S(1)}, u32[]{:S(2)}, u32[]{:S(2)}) async-start(bf16[8,48,1024]{2,1,0:T(8,128)(2,1)} %bitcast.6), calls=%async_computation | async-start | bytes 1572864 | tf_op jit(solution)/shard_map/all_to_all | solution.py:70
  46.3 6.3 %collective-permute-start.1 = (bf16[384,1024]{1,0:T(8,128)(2,1)S(1)}, bf16[384,1024]{1,0:T(8,128)(2,1)S(1)}, u32[]{:S(2)}, u32[]{:S(2)}) collective-permute-start(bf16[384,1024]{1,0:T(8,128)(2,1)S(1)} %bitcast.35), channel_id=1, source_target_pairs={{0,1},{1,0},{2,3},{3,2},{4,5},{5,4},{6,7},{7,6},{8,9},{9,8},{10,11... | collective-permute-start | bytes 2359304 | tf_op jit(solution)/shard_map/ppermute | solution.py:30
  50.6 1.9 %copy-start.8 = (bf16[512,1024]{1,0:T(8,128)(2,1)S(1)}, bf16[512,1024]{1,0:T(8,128)(2,1)}, u32[]{:S(2)}) copy-start(bf16[512,1024]{1,0:T(8,128)(2,1)} %param.10) | copy-start | bytes 3145732
  52.6 1.6 %copy-start.4 = (bf16[384,1024]{1,0:T(8,128)(2,1)}, bf16[384,1024]{1,0:T(8,128)(2,1)S(1)}, u32[]{:S(2)}) copy-start(bf16[384,1024]{1,0:T(8,128)(2,1)S(1)} %collective-permute-done.1) | copy-start | bytes 2359300
  54.2 33.9 %all-to-all-start.2 = ((bf16[32,24,512]{2,1,0:T(8,128)(2,1)}), bf16[32,24,512]{2,1,0:T(8,128)(2,1)S(1)}, u32[]{:S(2)}, u32[]{:S(2)}) async-start(bf16[32,24,512]{2,1,0:T(8,128)(2,1)} %bitcast.15), calls=%async_computation.2 | async-start | bytes 1572864 | tf_op jit(solution)/shard_map/all_to_all | solution.py:83
  65.5 17.7 %copy-start.2 = (bf16[8,1,48,512]{3,2,1,0:T(8,128)(2,1)S(1)}, bf16[8,1,48,512]{3,2,1,0:T(8,128)(2,1)}, u32[]{:S(2)}) copy-start(bf16[8,1,48,512]{3,2,1,0:T(8,128)(2,1)} %get-tuple-element.27) | copy-start | bytes 1179652
  65.5 17.7 %copy-start.5 = (bf16[384,1024]{1,0:T(8,128)(2,1)S(1)}, bf16[384,1024]{1,0:T(8,128)(2,1)}, u32[]{:S(2)}) copy-start(bf16[384,1024]{1,0:T(8,128)(2,1)} %copy-done.4) | copy-start | bytes 2359300
  77.2 8.7 %collective-permute-start.2 = (bf16[384,1024]{1,0:T(8,128)(2,1)S(1)}, bf16[384,1024]{1,0:T(8,128)(2,1)S(1)}, u32[]{:S(2)}, u32[]{:S(2)}) collective-permute-start(bf16[384,1024]{1,0:T(8,128)(2,1)S(1)} %all_gather.7), channel_id=1, source_target_pairs={{0,1},{1,0},{2,3},{3,2},{4,5},{5,4},{6,7},{7,6},{8,9},{9,8},{10,11... | collective-permute-start | bytes 2359304 | tf_op jit(solution)/shard_map/ppermute | solution.py:30
  83.2 1.0 %copy-start.1 = (bf16[8,1,48,512]{3,2,1,0:T(8,128)(2,1)S(1)}, bf16[8,1,48,512]{3,2,1,0:T(8,128)(2,1)}, u32[]{:S(2)}) copy-start(bf16[8,1,48,512]{3,2,1,0:T(8,128)(2,1)} %get-tuple-element.28) | copy-start | bytes 1179652

commit v4 on v3

--- a/solution.py
+++ b/solution.py
@@ -2,6 +2,7 @@
 
 import jax
 import jax.numpy as jnp
+import numpy as np
 from jax import lax
 from jax.sharding import Mesh
 from jax.sharding import PartitionSpec as P
@@ -24,6 +25,11 @@
     return lax.dot_general(
         left, right, (((0,), (0,)), ((), ())), preferred_element_type=jnp.float32
     )
+
+
+def listed_sections():
+    index = np.arange(512).reshape(8, 4, 16)[::-1, ::-1]
+    return index.reshape(32, 16).T.tolist()
 
 
 def core_swap(block):
@@ -79,8 +85,11 @@
         contract_last(mine, w_in).astype(jnp.bfloat16),
         contract_last(other, w_in).astype(jnp.bfloat16),
     )
+    partial = partial.reshape(8, 4, 24, 512)[::-1, ::-1].reshape(768, 512)
     hidden_pair, partial = lax.optimization_barrier((hidden_pair, partial))
-    blocks = lax.all_to_all(partial, SECTION, 0, 0, tiled=True)
+    blocks = lax.all_to_all(
+        partial, SECTION + DP, 0, 0, tiled=True, axis_index_groups=listed_sections()
+    )
     input_grad = jnp.sum(blocks.reshape(32, 24, 512).astype(jnp.float32), axis=0)
 
     hidden_mine = lax.all_gather(hidden_pair, "x", axis=0, tiled=True)

time: 90.6 us -> 89.6 us (0.989); the launches traced: 88.8 us -> 89.1 us
  local copies, waits for them, and re-layouts: 2.78 us -> 4.01 us
  other arithmetic: 3.2 us -> 2.29 us
    rev x0 -> x1, local copies, waits for them, and re-layouts: none -> 0.98 us  [body(): partial = partial.reshape(8, 4, 24, 512)[::-1, ::-1].reshape(768, 512)]
    another operation x1, other arithmetic: 0.99 us -> 0.08 us  [join_cores(): jnp.stack([jnp.where(first, mine, other), jnp.where(first, other, mine)],...]
  transfers between devices with their start and end apart: 5 -> 5, of which waited for: 2 -> 1; matrix products, arithmetic and copies ran while one was open for 10% -> 10% of each run, Pallas kernels for 0% -> 0%
where the time goes in v4:
time: 89.6 us; the launch traced here: 89.1 us
  blocking collectives  39.4 us (44%)
  starting transfers between devices  33.6 us (38%)
  matrix products  8.66 us (10%)
  local copies, waits for them, and re-layouts  4.01 us (4%)
  other arithmetic  2.29 us (3%)
    ppermute x3, starting transfers between devices, core_swap(): return lax.ppermute(block, 'core', [(0, 1), (1, 0)])  18.6 us
    all_to_all x1, blocking collectives, copies_to_chips(): return lax.all_to_all(jnp.tile(block, (8, 1)), CHIPS, 0, 0, tiled=True)  15.3 us
    all_gather x1, blocking collectives, body(): hidden_pair = lax.all_gather(hidden_own, 'zl', axis=0, tiled=True)  12.5 us
    all_gather x1, blocking collectives, body(): hidden_mine = lax.all_gather(hidden_pair, 'x', axis=0, tiled=True)  11.7 us
    all_to_all x1, starting transfers between devices, body(): lax.all_to_all(partial, SECTION + DP, 0, 0, tiled=True, axis_index_groups...  11.4 us
    dot_general x4, matrix products, contract_first(): lax.dot_general(left, right, (((0,), (0,)), ((), ())), preferred_element_...  4.93 us
    dot_general x4, matrix products, contract_last(): lax.dot_general(left, right, (((1,), (1,)), ((), ())), preferred_element_...  3.73 us
    all_to_all x1, starting transfers between devices, body(): lax.all_to_all(chip_sum.astype(jnp.bfloat16), CHIPS, 0, 0, tiled=True)  3.55 us
  transfers between devices with their start and end apart: 5, of which 1 were waited for; matrix products, arithmetic and copies ran while one was open for 10% of the time, Pallas kernels for 0%

profile of v4, /device:TPU:1, one launch (start us, length us, event | category | flops | bytes accessed | tf_op | source)
XLA Modules:
  0.0 89.1 jit_solution(9158083106650260613)
XLA Ops:
  0.7 1.3 %constant_dynamic-slice_fusion.3 = (bf16[8,1,48,512]{3,2,1,0:T(8,128)(2,1)S(1)}, bf16[8,1,48,512]{3,2,1,0:T(8,128)(2,1)S(1)}) fusion(bf16[8,2,48,512]{3,2,1,0:T(8,128)(2,1)} %bitcast.46, s32[]{:T(128)S(6)} %select_n.41, s32[]{:T(128)S(6)} %select_n.42), kind=kLoop, calls=%fused_computation.24 | loop fusion | bytes 1572872 | tf_op jit(solution)/shard_map/jit(dynamic_index_in_dim)/dynamic_slice | solution.py:42
  2.1 0.6 convolution_convert_fusion
  2.7 8.8 %collective-permute-start = (bf16[384,1024]{1,0:T(8,128)(2,1)S(1)}, bf16[384,1024]{1,0:T(8,128)(2,1)S(1)}, u32[]{:S(2)}, u32[]{:S(2)}) collective-permute-start(bf16[384,1024]{1,0:T(8,128)(2,1)S(1)} %convolution_convert_fusion), channel_id=1, source_target_pairs={{0,1},{1,0},{2,3},{3,2},{4,5},{5,4},{6,7},{7,6},{8,9},{9,8},{10,11... | collective-permute-start | bytes 2359304 | tf_op jit(solution)/shard_map/ppermute | solution.py:36
  11.5 0.6 convolution_convert_fusion.1
  12.1 1.0 %constant_dynamic-slice_fusion = (bf16[8,1,48,512]{3,2,1,0:T(8,128)(2,1)}, bf16[8,1,48,512]{3,2,1,0:T(8,128)(2,1)}) fusion(bf16[8,2,48,512]{3,2,1,0:T(8,128)(2,1)S(1)} %bitcast.47, s32[]{:T(128)S(6)} %select_n.42, s32[]{:T(128)S(6)} %select_n.41), kind=kLoop, calls=%fused_computation.21 | loop fusion | bytes 1572872 | tf_op jit(solution)/shard_map/jit(dynamic_index_in_dim)/dynamic_slice | solution.py:43
  13.1 0.3 collective-permute-done
  13.4 1.2 %add_convert_fusion.2 = bf16[384,1024]{1,0:T(8,128)(2,1)} fusion(bf16[384,1024]{1,0:T(8,128)(2,1)S(1)} %collective-permute-done, bf16[384,1024]{1,0:T(8,128)(2,1)S(1)} %convolution_convert_fusion.1), kind=kLoop, calls=%fused_computation.3 | loop fusion | flops 1572864 | bytes 2359296 | tf_op jit(solution)/shard_map/convert_element_type | solution.py:76
  14.6 3.5 %all-to-all-start = ((bf16[8,48,1024]{2,1,0:T(8,128)(2,1)}), bf16[8,48,1024]{2,1,0:T(8,128)(2,1)S(1)}, u32[]{:S(2)}, u32[]{:S(2)}) async-start(bf16[8,48,1024]{2,1,0:T(8,128)(2,1)} %bitcast.6), calls=%async_computation | async-start | bytes 1572864 | tf_op jit(solution)/shard_map/all_to_all | solution.py:76
  18.3 12.5 %all_gather.6 = bf16[96,1024]{1,0:T(8,128)(2,1)} all-gather(bf16[48,1024]{1,0:T(8,128)(2,1)S(1)} %get-tuple-element.16), channel_id=1, replica_groups=mesh['y'=8,'zh'=4,'x'=4,'zl'=2,'core'=2] {'zl'}, dimensions={0}, use_global_device_ids=true | all-gather | bytes 294912 | tf_op jit(solution)/shard_map/all_gather | solution.py:77
  31.0 15.3 %all_to_all.30 = bf16[8,48,1024]{2,1,0:T(8,128)(2,1)S(1)} all-to-all(bf16[8,48,1024]{2,1,0:T(8,128)(2,1)S(1)} %tile.2), channel_id=1, replica_groups=mesh['y'=8,'zh'=4,'x'=4,'zl'=2,'core'=2] {'x','zl'}, dimensions={0} | all-to-all | bytes 1572864 | tf_op jit(solution)/shard_map/all_to_all | solution.py:55
  46.3 4.3 %collective-permute-start.1 = (bf16[384,1024]{1,0:T(8,128)(2,1)S(1)}, bf16[384,1024]{1,0:T(8,128)(2,1)S(1)}, u32[]{:S(2)}, u32[]{:S(2)}) collective-permute-start(bf16[384,1024]{1,0:T(8,128)(2,1)S(1)} %bitcast.37), channel_id=1, source_target_pairs={{0,1},{1,0},{2,3},{3,2},{4,5},{5,4},{6,7},{7,6},{8,9},{9,8},{10,11... | collective-permute-start | bytes 2359304 | tf_op jit(solution)/shard_map/ppermute | solution.py:36
  50.6 1.9 %convolution_convert_fusion.3 = bf16[384,512]{1,0:T(8,128)(2,1)S(1)} fusion(bf16[384,1024]{1,0:T(8,128)(2,1)S(1)} %bitcast.38, bf16[512,1024]{1,0:T(8,128)(2,1)} %param.10), kind=kOutput, calls=%fused_computation.7 | convolution fusion | flops 402849792 | bytes 2228224 | tf_op jit(solution)/shard_map/dot_general | solution.py:19
  52.6 0.6 broadcast_select_fusion.1
  53.2 0.3 copy-done.4
  53.5 1.0 %rev.3 = bf16[8,4,24,512]{3,2,1,0:T(8,128)(2,1)} reverse(bf16[8,4,24,512]{3,2,1,0:T(8,128)(2,1)S(1)} %bitcast.36), dimensions={0,1} | reverse | bytes 1572864 | tf_op jit(solution)/shard_map/rev | solution.py:88
  54.5 11.4 %all-to-all-start.2 = ((bf16[32,24,512]{2,1,0:T(8,128)(2,1)}), bf16[32,24,512]{2,1,0:T(8,128)(2,1)S(1)}, u32[]{:S(2)}, u32[]{:S(2)}) async-start(bf16[32,24,512]{2,1,0:T(8,128)(2,1)} %bitcast.16), calls=%async_computation.2 | async-start | bytes 1572864 | tf_op jit(solution)/shard_map/all_to_all | solution.py:90
  66.0 11.7 %all_gather.7 = bf16[384,1024]{1,0:T(8,128)(2,1)S(1)} all-gather(bf16[96,1024]{1,0:T(8,128)(2,1)} %all_gather.6), channel_id=1, replica_groups=mesh['y'=8,'zh'=4,'x'=4,'zl'=2,'core'=2] {'x'}, dimensions={0}, use_global_device_ids=true | all-gather | bytes 983040 | tf_op jit(solution)/shard_map/all_gather | solution.py:95
  77.6 5.5 %collective-permute-start.2 = (bf16[384,1024]{1,0:T(8,128)(2,1)S(1)}, bf16[384,1024]{1,0:T(8,128)(2,1)S(1)}, u32[]{:S(2)}, u32[]{:S(2)}) collective-permute-start(bf16[384,1024]{1,0:T(8,128)(2,1)S(1)} %all_gather.7), channel_id=1, source_target_pairs={{0,1},{1,0},{2,3},{3,2},{4,5},{5,4},{6,7},{7,6},{8,9},{9,8},{10,11... | collective-permute-start | bytes 2359304 | tf_op jit(solution)/shard_map/ppermute | solution.py:36
  83.1 0.8 fusion.6
  83.9 0.7 fusion.5
  84.6 0.3 copy-done.1
  84.9 1.7 %add_convert_fusion.1 = bf16[512,1024]{1,0:T(8,128)(2,1)} fusion(f32[512,1024]{1,0:T(8,128)S(1)} %fusion.5, bf16[384,512]{1,0:T(8,128)(2,1)S(1)} %bitcast.44, bf16[384,1024]{1,0:T(8,128)(2,1)S(1)} %bitcast.39), kind=kOutput, calls=%fused_computation.1 | convolution fusion | flops 403701760 | bytes 4325376 | tf_op jit(solution)/shard_map/dot_general | solution.py:25
  86.6 1.7 %add_convert_fusion = bf16[1024,512]{1,0:T(8,128)(2,1)} fusion(f32[1024,512]{1,0:T(8,128)S(1)} %fusion.6, bf16[384,1024]{1,0:T(8,128)(2,1)S(1)} %collective-permute-done.2, bf16[384,512]{1,0:T(8,128)(2,1)S(1)} %bitcast.41), kind=kOutput, calls=%fused_computation | convolution fusion | flops 403701760 | bytes 4325376 | tf_op jit(solution)/shard_map/dot_general | solution.py:25
  88.3 0.7 reduce_sum.22
  (25 shorter events, 0.7 us)
Async XLA Ops:
  0.6 1.5 %copy-start = (bf16[1024,512]{1,0:T(8,128)(2,1)S(1)}, bf16[1024,512]{1,0:T(8,128)(2,1)}, u32[]{:S(2)}) copy-start(bf16[1024,512]{1,0:T(8,128)(2,1)} %param.11) | copy-start | bytes 3145732
  2.1 10.0 %copy-start.3 = (bf16[768,512]{1,0:T(8,128)(2,1)S(1)}, bf16[768,512]{1,0:T(8,128)(2,1)}, u32[]{:S(2)}) copy-start(bf16[768,512]{1,0:T(8,128)(2,1)} %param.6) | copy-start | bytes 2359300
  2.7 10.7 %collective-permute-start = (bf16[384,1024]{1,0:T(8,128)(2,1)S(1)}, bf16[384,1024]{1,0:T(8,128)(2,1)S(1)}, u32[]{:S(2)}, u32[]{:S(2)}) collective-permute-start(bf16[384,1024]{1,0:T(8,128)(2,1)S(1)} %convolution_convert_fusion), channel_id=1, source_target_pairs={{0,1},{1,0},{2,3},{3,2},{4,5},{5,4},{6,7},{7,6},{8,9},{9,8},{10,11... | collective-permute-start | bytes 2359304 | tf_op jit(solution)/shard_map/ppermute | solution.py:36
  13.1 5.1 %copy-start.6 = (s32[48,1024]{1,0:T(8,128)S(1)}, s32[48,1024]{1,0:T(8,128)}, u32[]{:S(2)}) copy-start(s32[48,1024]{1,0:T(8,128)} %param.8) | copy-start | bytes 589828
  13.1 5.1 %copy-start.7 = (f32[48]{0:T(128)S(1)}, f32[48]{0:T(128)}, u32[]{:S(2)}) copy-start(f32[48]{0:T(128)} %param.9) | copy-start | bytes 580
  14.6 16.2 %all-to-all-start = ((bf16[8,48,1024]{2,1,0:T(8,128)(2,1)}), bf16[8,48,1024]{2,1,0:T(8,128)(2,1)S(1)}, u32[]{:S(2)}, u32[]{:S(2)}) async-start(bf16[8,48,1024]{2,1,0:T(8,128)(2,1)} %bitcast.6), calls=%async_computation | async-start | bytes 1572864 | tf_op jit(solution)/shard_map/all_to_all | solution.py:76
  46.3 6.3 %collective-permute-start.1 = (bf16[384,1024]{1,0:T(8,128)(2,1)S(1)}, bf16[384,1024]{1,0:T(8,128)(2,1)S(1)}, u32[]{:S(2)}, u32[]{:S(2)}) collective-permute-start(bf16[384,1024]{1,0:T(8,128)(2,1)S(1)} %bitcast.37), channel_id=1, source_target_pairs={{0,1},{1,0},{2,3},{3,2},{4,5},{5,4},{6,7},{7,6},{8,9},{9,8},{10,11... | collective-permute-start | bytes 2359304 | tf_op jit(solution)/shard_map/ppermute | solution.py:36
  50.6 1.9 %copy-start.8 = (bf16[512,1024]{1,0:T(8,128)(2,1)S(1)}, bf16[512,1024]{1,0:T(8,128)(2,1)}, u32[]{:S(2)}) copy-start(bf16[512,1024]{1,0:T(8,128)(2,1)} %param.10) | copy-start | bytes 3145732
  52.6 0.9 copy-start.4
  54.5 33.8 %all-to-all-start.2 = ((bf16[32,24,512]{2,1,0:T(8,128)(2,1)}), bf16[32,24,512]{2,1,0:T(8,128)(2,1)S(1)}, u32[]{:S(2)}, u32[]{:S(2)}) async-start(bf16[32,24,512]{2,1,0:T(8,128)(2,1)} %bitcast.16), calls=%async_computation.2 | async-start | bytes 1572864 | tf_op jit(solution)/shard_map/all_to_all | solution.py:90
  65.9 18.0 %copy-start.2 = (bf16[8,1,48,512]{3,2,1,0:T(8,128)(2,1)S(1)}, bf16[8,1,48,512]{3,2,1,0:T(8,128)(2,1)}, u32[]{:S(2)}) copy-start(bf16[8,1,48,512]{3,2,1,0:T(8,128)(2,1)} %get-tuple-element.27) | copy-start | bytes 1179652
  65.9 18.0 %copy-start.5 = (bf16[384,1024]{1,0:T(8,128)(2,1)S(1)}, bf16[384,1024]{1,0:T(8,128)(2,1)}, u32[]{:S(2)}) copy-start(bf16[384,1024]{1,0:T(8,128)(2,1)} %copy-done.4) | copy-start | bytes 2359300
  77.6 9.0 %collective-permute-start.2 = (bf16[384,1024]{1,0:T(8,128)(2,1)S(1)}, bf16[384,1024]{1,0:T(8,128)(2,1)S(1)}, u32[]{:S(2)}, u32[]{:S(2)}) collective-permute-start(bf16[384,1024]{1,0:T(8,128)(2,1)S(1)} %all_gather.7), channel_id=1, source_target_pairs={{0,1},{1,0},{2,3},{3,2},{4,5},{5,4},{6,7},{7,6},{8,9},{9,8},{10,11... | collective-permute-start | bytes 2359304 | tf_op jit(solution)/shard_map/ppermute | solution.py:36
  83.9 1.0 %copy-start.1 = (bf16[8,1,48,512]{3,2,1,0:T(8,128)(2,1)S(1)}, bf16[8,1,48,512]{3,2,1,0:T(8,128)(2,1)}, u32[]{:S(2)}) copy-start(bf16[8,1,48,512]{3,2,1,0:T(8,128)(2,1)} %get-tuple-element.28) | copy-start | bytes 1179652

commit v5 on v4

--- a/solution.py
+++ b/solution.py
@@ -69,17 +69,17 @@
     own_sum = lax.optimization_barrier(contract_last(grad_mine, w_out).astype(jnp.bfloat16))
     inputs, grad_mine = lax.optimization_barrier((inputs, grad_mine))
     inputs_mine, inputs_other = split_cores(inputs)
-    received, inputs_mine, inputs_other = lax.optimization_barrier(
-        (received, inputs_mine, inputs_other)
+    received, inputs_mine, inputs_other, hidden_own, slope_own = lax.optimization_barrier(
+        (received, inputs_mine, inputs_other, hidden_own, slope_own)
     )
     chip_sum = own_sum.astype(jnp.float32) + received.astype(jnp.float32)
     blocks = lax.all_to_all(chip_sum.astype(jnp.bfloat16), CHIPS, 0, 0, tiled=True)
-    hidden_pair = lax.all_gather(hidden_own, "zl", axis=0, tiled=True)
-    blocks, hidden_pair = lax.optimization_barrier((blocks, hidden_pair))
     grad_share = jnp.sum(blocks.reshape(8, 48, 1024).astype(jnp.float32), axis=0)
     pre_grad_own = (grad_share * slope_own).astype(jnp.bfloat16)
 
     mine = copies_to_chips(pre_grad_own)
+    hidden_pair = lax.all_gather(hidden_own, "zl", axis=0, tiled=True)
+    mine, hidden_pair = lax.optimization_barrier((mine, hidden_pair))
     other = core_swap(mine)
     partial = join_cores(
         contract_last(mine, w_in).astype(jnp.bfloat16),

time: 89.6 us -> 89.2 us (level)
  blocking collectives: 39.4 us -> 38.5 us
where the time goes in v5:
time: 89.2 us; the launch traced here: 88.7 us
  blocking collectives  38.5 us (43%)
  starting transfers between devices  34.2 us (38%)
  matrix products  8.64 us (10%)
  local copies, waits for them, and re-layouts  4.88 us (5%)
  other arithmetic  1.41 us (2%)
    ppermute x3, starting transfers between devices, core_swap(): return lax.ppermute(block, 'core', [(0, 1), (1, 0)])  18.5 us
    all_to_all x1, blocking collectives, body(): lax.all_to_all(chip_sum.astype(jnp.bfloat16), CHIPS, 0, 0, tiled=True)  15.1 us
    all_to_all x1, starting transfers between devices, body(): lax.all_to_all(partial, SECTION + DP, 0, 0, tiled=True, axis_index_groups...  12.2 us
    all_gather x1, blocking collectives, body(): hidden_mine = lax.all_gather(hidden_pair, 'x', axis=0, tiled=True)  11.9 us
    all_gather x1, blocking collectives, body(): hidden_pair = lax.all_gather(hidden_own, 'zl', axis=0, tiled=True)  11.6 us
    dot_general x4, matrix products, contract_first(): lax.dot_general(left, right, (((0,), (0,)), ((), ())), preferred_element_...  4.92 us
    dot_general x4, matrix products, contract_last(): lax.dot_general(left, right, (((1,), (1,)), ((), ())), preferred_element_...  3.72 us
    all_to_all x1, starting transfers between devices, copies_to_chips(): return lax.all_to_all(jnp.tile(block, (8, 1)), CHIPS, 0, 0, tiled=True)  3.55 us
  transfers between devices with their start and end apart: 5, of which 1 were waited for; matrix products, arithmetic and copies ran while one was open for 10% of the time, Pallas kernels for 0%

profile of v5, /device:TPU:1, one launch (start us, length us, event | category | flops | bytes accessed | tf_op | source)
XLA Modules:
  0.0 88.7 jit_solution(2217181474338198564)
XLA Ops:
  0.7 1.3 %constant_dynamic-slice_fusion.3 = (bf16[8,1,48,512]{3,2,1,0:T(8,128)(2,1)S(1)}, bf16[8,1,48,512]{3,2,1,0:T(8,128)(2,1)S(1)}) fusion(bf16[8,2,48,512]{3,2,1,0:T(8,128)(2,1)} %bitcast.44, s32[]{:T(128)S(6)} %select_n.41, s32[]{:T(128)S(6)} %select_n.42), kind=kLoop, calls=%fused_computation.24 | loop fusion | bytes 1572872 | tf_op jit(solution)/shard_map/jit(dynamic_index_in_dim)/dynamic_slice | solution.py:42
  2.1 0.6 convolution_convert_fusion
  2.7 8.8 %collective-permute-start = (bf16[384,1024]{1,0:T(8,128)(2,1)S(1)}, bf16[384,1024]{1,0:T(8,128)(2,1)S(1)}, u32[]{:S(2)}, u32[]{:S(2)}) collective-permute-start(bf16[384,1024]{1,0:T(8,128)(2,1)S(1)} %convolution_convert_fusion), channel_id=1, source_target_pairs={{0,1},{1,0},{2,3},{3,2},{4,5},{5,4},{6,7},{7,6},{8,9},{9,8},{10,11... | collective-permute-start | bytes 2359304 | tf_op jit(solution)/shard_map/ppermute | solution.py:36
  11.7 0.6 convolution_convert_fusion.1
  12.3 1.0 %constant_dynamic-slice_fusion = (bf16[8,1,48,512]{3,2,1,0:T(8,128)(2,1)}, bf16[8,1,48,512]{3,2,1,0:T(8,128)(2,1)}) fusion(bf16[8,2,48,512]{3,2,1,0:T(8,128)(2,1)S(1)} %bitcast.45, s32[]{:T(128)S(6)} %select_n.42, s32[]{:T(128)S(6)} %select_n.41), kind=kLoop, calls=%fused_computation.21 | loop fusion | bytes 1572872 | tf_op jit(solution)/shard_map/jit(dynamic_index_in_dim)/dynamic_slice | solution.py:43
  13.4 0.3 add_convert_fusion.2
  13.7 15.1 %all_to_all.27 = bf16[8,48,1024]{2,1,0:T(8,128)(2,1)S(1)} all-to-all(bf16[8,48,1024]{2,1,0:T(8,128)(2,1)S(1)} %bitcast.34), channel_id=1, replica_groups=mesh['y'=8,'zh'=4,'x'=4,'zl'=2,'core'=2] {'x','zl'}, dimensions={0} | all-to-all | bytes 1572864 | tf_op jit(solution)/shard_map/all_to_all | solution.py:76
  28.9 1.0 %tile.2 = bf16[8,48,1024]{2,1,0:T(8,128)(2,1)} broadcast(bf16[48,1024]{1,0:T(8,128)(2,1)S(1)} %multiply_convert_fusion), dimensions={1,2} | broadcast | bytes 884736 | tf_op jit(solution)/shard_map/tile | solution.py:55
  29.9 3.5 %all-to-all-start.1 = ((bf16[8,48,1024]{2,1,0:T(8,128)(2,1)}), bf16[8,48,1024]{2,1,0:T(8,128)(2,1)S(1)}, u32[]{:S(2)}, u32[]{:S(2)}) async-start(bf16[8,48,1024]{2,1,0:T(8,128)(2,1)} %tile.2), calls=%async_computation.1 | async-start | bytes 1572864 | tf_op jit(solution)/shard_map/all_to_all | solution.py:55
  33.4 11.6 %all_gather.6 = bf16[96,1024]{1,0:T(8,128)(2,1)} all-gather(bf16[48,1024]{1,0:T(8,128)(2,1)S(1)} %get-tuple-element.21), channel_id=1, replica_groups=mesh['y'=8,'zh'=4,'x'=4,'zl'=2,'core'=2] {'zl'}, dimensions={0}, use_global_device_ids=true | all-gather | bytes 294912 | tf_op jit(solution)/shard_map/all_gather | solution.py:81
  45.1 5.1 %collective-permute-start.1 = (bf16[384,1024]{1,0:T(8,128)(2,1)S(1)}, bf16[384,1024]{1,0:T(8,128)(2,1)S(1)}, u32[]{:S(2)}, u32[]{:S(2)}) collective-permute-start(bf16[384,1024]{1,0:T(8,128)(2,1)S(1)} %bitcast.35), channel_id=1, source_target_pairs={{0,1},{1,0},{2,3},{3,2},{4,5},{5,4},{6,7},{7,6},{8,9},{9,8},{10,11... | collective-permute-start | bytes 2359304 | tf_op jit(solution)/shard_map/ppermute | solution.py:36
  50.2 1.9 %convolution_convert_fusion.3 = bf16[384,512]{1,0:T(8,128)(2,1)S(1)} fusion(bf16[384,1024]{1,0:T(8,128)(2,1)S(1)} %bitcast.36, bf16[512,1024]{1,0:T(8,128)(2,1)} %param.10), kind=kOutput, calls=%fused_computation.7 | convolution fusion | flops 402849792 | bytes 2228224 | tf_op jit(solution)/shard_map/dot_general | solution.py:19
  52.2 0.6 broadcast_select_fusion.1
  52.8 0.3 copy-done.4
  53.1 1.0 %rev.3 = bf16[8,4,24,512]{3,2,1,0:T(8,128)(2,1)} reverse(bf16[8,4,24,512]{3,2,1,0:T(8,128)(2,1)S(1)} %bitcast.33), dimensions={0,1} | reverse | bytes 1572864 | tf_op jit(solution)/shard_map/rev | solution.py:88
  54.1 12.2 %all-to-all-start.2 = ((bf16[32,24,512]{2,1,0:T(8,128)(2,1)}), bf16[32,24,512]{2,1,0:T(8,128)(2,1)S(1)}, u32[]{:S(2)}, u32[]{:S(2)}) async-start(bf16[32,24,512]{2,1,0:T(8,128)(2,1)} %bitcast.14), calls=%async_computation.2 | async-start | bytes 1572864 | tf_op jit(solution)/shard_map/all_to_all | solution.py:90
  66.3 11.9 %all_gather.7 = bf16[384,1024]{1,0:T(8,128)(2,1)S(1)} all-gather(bf16[96,1024]{1,0:T(8,128)(2,1)} %all_gather.6), channel_id=1, replica_groups=mesh['y'=8,'zh'=4,'x'=4,'zl'=2,'core'=2] {'x'}, dimensions={0}, use_global_device_ids=true | all-gather | bytes 983040 | tf_op jit(solution)/shard_map/all_gather | solution.py:95
  78.2 4.6 %collective-permute-start.2 = (bf16[384,1024]{1,0:T(8,128)(2,1)S(1)}, bf16[384,1024]{1,0:T(8,128)(2,1)S(1)}, u32[]{:S(2)}, u32[]{:S(2)}) collective-permute-start(bf16[384,1024]{1,0:T(8,128)(2,1)S(1)} %all_gather.7), channel_id=1, source_target_pairs={{0,1},{1,0},{2,3},{3,2},{4,5},{5,4},{6,7},{7,6},{8,9},{9,8},{10,11... | collective-permute-start | bytes 2359304 | tf_op jit(solution)/shard_map/ppermute | solution.py:36
  82.7 0.8 fusion.6
  83.5 0.7 fusion.5
  84.2 0.3 copy-done.1
  84.5 1.7 %add_convert_fusion.1 = bf16[512,1024]{1,0:T(8,128)(2,1)} fusion(f32[512,1024]{1,0:T(8,128)S(1)} %fusion.5, bf16[384,512]{1,0:T(8,128)(2,1)S(1)} %bitcast.42, bf16[384,1024]{1,0:T(8,128)(2,1)S(1)} %bitcast.37), kind=kOutput, calls=%fused_computation.1 | convolution fusion | flops 403701760 | bytes 4325376 | tf_op jit(solution)/shard_map/dot_general | solution.py:25
  86.2 1.7 %add_convert_fusion = bf16[1024,512]{1,0:T(8,128)(2,1)} fusion(f32[1024,512]{1,0:T(8,128)S(1)} %fusion.6, bf16[384,1024]{1,0:T(8,128)(2,1)S(1)} %collective-permute-done.2, bf16[384,512]{1,0:T(8,128)(2,1)S(1)} %bitcast.39), kind=kOutput, calls=%fused_computation | convolution fusion | flops 403701760 | bytes 4325376 | tf_op jit(solution)/shard_map/dot_general | solution.py:25
  87.9 0.7 reduce_sum.22
  (25 shorter events, 0.7 us)
Async XLA Ops:
  0.6 1.5 %copy-start = (bf16[1024,512]{1,0:T(8,128)(2,1)S(1)}, bf16[1024,512]{1,0:T(8,128)(2,1)}, u32[]{:S(2)}) copy-start(bf16[1024,512]{1,0:T(8,128)(2,1)} %param.11) | copy-start | bytes 3145732
  0.6 10.9 %copy-start.6 = (s32[48,1024]{1,0:T(8,128)S(1)}, s32[48,1024]{1,0:T(8,128)}, u32[]{:S(2)}) copy-start(s32[48,1024]{1,0:T(8,128)} %param.8) | copy-start | bytes 589828
  0.7 10.9 %copy-start.7 = (f32[48]{0:T(128)S(1)}, f32[48]{0:T(128)}, u32[]{:S(2)}) copy-start(f32[48]{0:T(128)} %param.9) | copy-start | bytes 580
  2.1 10.2 %copy-start.3 = (bf16[768,512]{1,0:T(8,128)(2,1)S(1)}, bf16[768,512]{1,0:T(8,128)(2,1)}, u32[]{:S(2)}) copy-start(bf16[768,512]{1,0:T(8,128)(2,1)} %param.6) | copy-start | bytes 2359300
  2.7 10.7 %collective-permute-start = (bf16[384,1024]{1,0:T(8,128)(2,1)S(1)}, bf16[384,1024]{1,0:T(8,128)(2,1)S(1)}, u32[]{:S(2)}, u32[]{:S(2)}) collective-permute-start(bf16[384,1024]{1,0:T(8,128)(2,1)S(1)} %convolution_convert_fusion), channel_id=1, source_target_pairs={{0,1},{1,0},{2,3},{3,2},{4,5},{5,4},{6,7},{7,6},{8,9},{9,8},{10,11... | collective-permute-start | bytes 2359304 | tf_op jit(solution)/shard_map/ppermute | solution.py:36
  29.9 15.2 %all-to-all-start.1 = ((bf16[8,48,1024]{2,1,0:T(8,128)(2,1)}), bf16[8,48,1024]{2,1,0:T(8,128)(2,1)S(1)}, u32[]{:S(2)}, u32[]{:S(2)}) async-start(bf16[8,48,1024]{2,1,0:T(8,128)(2,1)} %tile.2), calls=%async_computation.1 | async-start | bytes 1572864 | tf_op jit(solution)/shard_map/all_to_all | solution.py:55
  45.1 7.1 %collective-permute-start.1 = (bf16[384,1024]{1,0:T(8,128)(2,1)S(1)}, bf16[384,1024]{1,0:T(8,128)(2,1)S(1)}, u32[]{:S(2)}, u32[]{:S(2)}) collective-permute-start(bf16[384,1024]{1,0:T(8,128)(2,1)S(1)} %bitcast.35), channel_id=1, source_target_pairs={{0,1},{1,0},{2,3},{3,2},{4,5},{5,4},{6,7},{7,6},{8,9},{9,8},{10,11... | collective-permute-start | bytes 2359304 | tf_op jit(solution)/shard_map/ppermute | solution.py:36
  50.2 1.9 %copy-start.8 = (bf16[512,1024]{1,0:T(8,128)(2,1)S(1)}, bf16[512,1024]{1,0:T(8,128)(2,1)}, u32[]{:S(2)}) copy-start(bf16[512,1024]{1,0:T(8,128)(2,1)} %param.10) | copy-start | bytes 3145732
  52.1 0.9 copy-start.4
  54.1 33.9 %all-to-all-start.2 = ((bf16[32,24,512]{2,1,0:T(8,128)(2,1)}), bf16[32,24,512]{2,1,0:T(8,128)(2,1)S(1)}, u32[]{:S(2)}, u32[]{:S(2)}) async-start(bf16[32,24,512]{2,1,0:T(8,128)(2,1)} %bitcast.14), calls=%async_computation.2 | async-start | bytes 1572864 | tf_op jit(solution)/shard_map/all_to_all | solution.py:90
  66.3 17.2 %copy-start.2 = (bf16[8,1,48,512]{3,2,1,0:T(8,128)(2,1)S(1)}, bf16[8,1,48,512]{3,2,1,0:T(8,128)(2,1)}, u32[]{:S(2)}) copy-start(bf16[8,1,48,512]{3,2,1,0:T(8,128)(2,1)} %get-tuple-element.31) | copy-start | bytes 1179652
  66.3 17.2 %copy-start.5 = (bf16[384,1024]{1,0:T(8,128)(2,1)S(1)}, bf16[384,1024]{1,0:T(8,128)(2,1)}, u32[]{:S(2)}) copy-start(bf16[384,1024]{1,0:T(8,128)(2,1)} %copy-done.4) | copy-start | bytes 2359300
  78.2 8.0 %collective-permute-start.2 = (bf16[384,1024]{1,0:T(8,128)(2,1)S(1)}, bf16[384,1024]{1,0:T(8,128)(2,1)S(1)}, u32[]{:S(2)}, u32[]{:S(2)}) collective-permute-start(bf16[384,1024]{1,0:T(8,128)(2,1)S(1)} %all_gather.7), channel_id=1, source_target_pairs={{0,1},{1,0},{2,3},{3,2},{4,5},{5,4},{6,7},{7,6},{8,9},{9,8},{10,11... | collective-permute-start | bytes 2359304 | tf_op jit(solution)/shard_map/ppermute | solution.py:36
  83.5 1.0 %copy-start.1 = (bf16[8,1,48,512]{3,2,1,0:T(8,128)(2,1)S(1)}, bf16[8,1,48,512]{3,2,1,0:T(8,128)(2,1)}, u32[]{:S(2)}) copy-start(bf16[8,1,48,512]{3,2,1,0:T(8,128)(2,1)} %get-tuple-element.32) | copy-start | bytes 1179652

commit v6 on v5

--- a/solution.py
+++ b/solution.py
@@ -51,10 +51,6 @@
     return both.reshape(768, -1)
 
 
-def copies_to_chips(block):
-    return lax.all_to_all(jnp.tile(block, (8, 1)), CHIPS, 0, 0, tiled=True)
-
-
 def body(inputs, out_grad, saved_codes, row_scale, w_in, w_out):
     pre_act = saved_codes.astype(jnp.float32) * row_scale[:, None]
     normal_cdf = 0.5 * (1.0 + jax.scipy.special.erf(pre_act * inv_root_two))
@@ -69,15 +65,16 @@
     own_sum = lax.optimization_barrier(contract_last(grad_mine, w_out).astype(jnp.bfloat16))
     inputs, grad_mine = lax.optimization_barrier((inputs, grad_mine))
     inputs_mine, inputs_other = split_cores(inputs)
-    received, inputs_mine, inputs_other, hidden_own, slope_own = lax.optimization_barrier(
-        (received, inputs_mine, inputs_other, hidden_own, slope_own)
+    slopes = jnp.broadcast_to(slope_own[None], (8, 48, 1024))
+    received, inputs_mine, inputs_other, hidden_own, slopes = lax.optimization_barrier(
+        (received, inputs_mine, inputs_other, hidden_own, slopes)
     )
     chip_sum = own_sum.astype(jnp.float32) + received.astype(jnp.float32)
     blocks = lax.all_to_all(chip_sum.astype(jnp.bfloat16), CHIPS, 0, 0, tiled=True)
     grad_share = jnp.sum(blocks.reshape(8, 48, 1024).astype(jnp.float32), axis=0)
-    pre_grad_own = (grad_share * slope_own).astype(jnp.bfloat16)
+    pre_grad_copies = (grad_share[None] * slopes).astype(jnp.bfloat16).reshape(384, 1024)
 
-    mine = copies_to_chips(pre_grad_own)
+    mine = lax.all_to_all(pre_grad_copies, CHIPS, 0, 0, tiled=True)
     hidden_pair = lax.all_gather(hidden_own, "zl", axis=0, tiled=True)
     mine, hidden_pair = lax.optimization_barrier((mine, hidden_pair))
     other = core_swap(mine)

time: 89.2 us -> 89.3 us (level)
  other arithmetic: 1.41 us -> 2.47 us
    convert_element_type x1, other arithmetic: 0.02 us -> 1.08 us  [body(): (grad_share[None] * slopes).astype(jnp.bfloat16).reshape(384, 1024)]
    another operation x1 -> x0, local copies, waits for them, and re-layouts: 0.97 us -> none  [copies_to_chips(): return lax.all_to_all(jnp.tile(block, (8, 1)), CHIPS, 0, 0, tiled=True)]
where the time goes in v6:
time: 89.3 us; the launch traced here: 88.8 us
  blocking collectives  38.5 us (43%)
  starting transfers between devices  34.2 us (38%)
  matrix products  8.64 us (10%)
  local copies, waits for them, and re-layouts  3.99 us (4%)
  other arithmetic  2.47 us (3%)
    ppermute x3, starting transfers between devices, core_swap(): return lax.ppermute(block, 'core', [(0, 1), (1, 0)])  18.5 us
    all_to_all x1, blocking collectives, body(): lax.all_to_all(chip_sum.astype(jnp.bfloat16), CHIPS, 0, 0, tiled=True)  15.1 us
    all_to_all x1, starting transfers between devices, body(): lax.all_to_all(partial, SECTION + DP, 0, 0, tiled=True, axis_index_groups...  12.2 us
    all_gather x1, blocking collectives, body(): hidden_mine = lax.all_gather(hidden_pair, 'x', axis=0, tiled=True)  11.9 us
    all_gather x1, blocking collectives, body(): hidden_pair = lax.all_gather(hidden_own, 'zl', axis=0, tiled=True)  11.6 us
    dot_general x4, matrix products, contract_first(): lax.dot_general(left, right, (((0,), (0,)), ((), ())), preferred_element_...  4.91 us
    dot_general x4, matrix products, contract_last(): lax.dot_general(left, right, (((1,), (1,)), ((), ())), preferred_element_...  3.73 us
    all_to_all x1, starting transfers between devices, body(): mine = lax.all_to_all(pre_grad_copies, CHIPS, 0, 0, tiled=True)  3.55 us
  transfers between devices with their start and end apart: 5, of which 1 were waited for; matrix products, arithmetic and copies ran while one was open for 10% of the time, Pallas kernels for 0%

profile of v6, /device:TPU:1, one launch (start us, length us, event | category | flops | bytes accessed | tf_op | source)
XLA Modules:
  0.0 88.8 jit_solution(11985242248103981730)
XLA Ops:
  0.7 1.3 %constant_dynamic-slice_fusion.3 = (bf16[8,1,48,512]{3,2,1,0:T(8,128)(2,1)S(1)}, bf16[8,1,48,512]{3,2,1,0:T(8,128)(2,1)S(1)}) fusion(bf16[8,2,48,512]{3,2,1,0:T(8,128)(2,1)} %bitcast.44, s32[]{:T(128)S(6)} %select_n.41, s32[]{:T(128)S(6)} %select_n.42), kind=kLoop, calls=%fused_computation.24 | loop fusion | bytes 1572872 | tf_op jit(solution)/shard_map/jit(dynamic_index_in_dim)/dynamic_slice | solution.py:42
  2.1 0.6 convolution_convert_fusion
  2.7 8.8 %collective-permute-start = (bf16[384,1024]{1,0:T(8,128)(2,1)S(1)}, bf16[384,1024]{1,0:T(8,128)(2,1)S(1)}, u32[]{:S(2)}, u32[]{:S(2)}) collective-permute-start(bf16[384,1024]{1,0:T(8,128)(2,1)S(1)} %convolution_convert_fusion), channel_id=1, source_target_pairs={{0,1},{1,0},{2,3},{3,2},{4,5},{5,4},{6,7},{7,6},{8,9},{9,8},{10,11... | collective-permute-start | bytes 2359304 | tf_op jit(solution)/shard_map/ppermute | solution.py:36
  11.7 0.6 convolution_convert_fusion.1
  12.3 1.0 %constant_dynamic-slice_fusion = (bf16[8,1,48,512]{3,2,1,0:T(8,128)(2,1)}, bf16[8,1,48,512]{3,2,1,0:T(8,128)(2,1)}) fusion(bf16[8,2,48,512]{3,2,1,0:T(8,128)(2,1)S(1)} %bitcast.45, s32[]{:T(128)S(6)} %select_n.42, s32[]{:T(128)S(6)} %select_n.41), kind=kLoop, calls=%fused_computation.21 | loop fusion | bytes 1572872 | tf_op jit(solution)/shard_map/jit(dynamic_index_in_dim)/dynamic_slice | solution.py:43
  13.5 0.3 add_convert_fusion.2
  13.8 15.1 %all_to_all.27 = bf16[8,48,1024]{2,1,0:T(8,128)(2,1)S(1)} all-to-all(bf16[8,48,1024]{2,1,0:T(8,128)(2,1)S(1)} %bitcast.34), channel_id=1, replica_groups=mesh['y'=8,'zh'=4,'x'=4,'zl'=2,'core'=2] {'x','zl'}, dimensions={0} | all-to-all | bytes 1572864 | tf_op jit(solution)/shard_map/all_to_all | solution.py:73
  29.0 1.1 %multiply_convert_fusion = bf16[8,48,1024]{2,1,0:T(8,128)(2,1)} fusion(bf16[8,48,1024]{2,1,0:T(8,128)(2,1)S(1)} %broadcast_in_dim.2, f32[48,1024]{1,0:T(8,128)S(1)} %convert_reduce_fusion), kind=kLoop, calls=%fused_computation.2 | loop fusion | flops 1179648 | bytes 1769472 | tf_op jit(solution)/shard_map/convert_element_type | solution.py:75
  30.1 3.5 %all-to-all-start.1 = ((bf16[8,48,1024]{2,1,0:T(8,128)(2,1)}), bf16[8,48,1024]{2,1,0:T(8,128)(2,1)S(1)}, u32[]{:S(2)}, u32[]{:S(2)}) async-start(bf16[8,48,1024]{2,1,0:T(8,128)(2,1)} %multiply_convert_fusion), calls=%async_computation.1 | async-start | bytes 1572864 | tf_op jit(solution)/shard_map/all_to_all | solution.py:77
  33.6 11.6 %all_gather.6 = bf16[96,1024]{1,0:T(8,128)(2,1)} all-gather(bf16[48,1024]{1,0:T(8,128)(2,1)S(1)} %get-tuple-element.21), channel_id=1, replica_groups=mesh['y'=8,'zh'=4,'x'=4,'zl'=2,'core'=2] {'zl'}, dimensions={0}, use_global_device_ids=true | all-gather | bytes 294912 | tf_op jit(solution)/shard_map/all_gather | solution.py:78
  45.2 5.1 %collective-permute-start.1 = (bf16[384,1024]{1,0:T(8,128)(2,1)S(1)}, bf16[384,1024]{1,0:T(8,128)(2,1)S(1)}, u32[]{:S(2)}, u32[]{:S(2)}) collective-permute-start(bf16[384,1024]{1,0:T(8,128)(2,1)S(1)} %bitcast.35), channel_id=1, source_target_pairs={{0,1},{1,0},{2,3},{3,2},{4,5},{5,4},{6,7},{7,6},{8,9},{9,8},{10,11... | collective-permute-start | bytes 2359304 | tf_op jit(solution)/shard_map/ppermute | solution.py:36
  50.4 1.9 %convolution_convert_fusion.3 = bf16[384,512]{1,0:T(8,128)(2,1)S(1)} fusion(bf16[384,1024]{1,0:T(8,128)(2,1)S(1)} %bitcast.36, bf16[512,1024]{1,0:T(8,128)(2,1)} %param.10), kind=kOutput, calls=%fused_computation.8 | convolution fusion | flops 402849792 | bytes 2228224 | tf_op jit(solution)/shard_map/dot_general | solution.py:19
  52.3 0.6 broadcast_select_fusion.1
  53.0 0.3 copy-done.4
  53.3 1.0 %rev.3 = bf16[8,4,24,512]{3,2,1,0:T(8,128)(2,1)} reverse(bf16[8,4,24,512]{3,2,1,0:T(8,128)(2,1)S(1)} %bitcast.33), dimensions={0,1} | reverse | bytes 1572864 | tf_op jit(solution)/shard_map/rev | solution.py:85
  54.3 12.2 %all-to-all-start.2 = ((bf16[32,24,512]{2,1,0:T(8,128)(2,1)}), bf16[32,24,512]{2,1,0:T(8,128)(2,1)S(1)}, u32[]{:S(2)}, u32[]{:S(2)}) async-start(bf16[32,24,512]{2,1,0:T(8,128)(2,1)} %bitcast.14), calls=%async_computation.2 | async-start | bytes 1572864 | tf_op jit(solution)/shard_map/all_to_all | solution.py:87
  66.5 11.9 %all_gather.7 = bf16[384,1024]{1,0:T(8,128)(2,1)S(1)} all-gather(bf16[96,1024]{1,0:T(8,128)(2,1)} %all_gather.6), channel_id=1, replica_groups=mesh['y'=8,'zh'=4,'x'=4,'zl'=2,'core'=2] {'x'}, dimensions={0}, use_global_device_ids=true | all-gather | bytes 983040 | tf_op jit(solution)/shard_map/all_gather | solution.py:92
  78.3 4.6 %collective-permute-start.2 = (bf16[384,1024]{1,0:T(8,128)(2,1)S(1)}, bf16[384,1024]{1,0:T(8,128)(2,1)S(1)}, u32[]{:S(2)}, u32[]{:S(2)}) collective-permute-start(bf16[384,1024]{1,0:T(8,128)(2,1)S(1)} %all_gather.7), channel_id=1, source_target_pairs={{0,1},{1,0},{2,3},{3,2},{4,5},{5,4},{6,7},{7,6},{8,9},{9,8},{10,11... | collective-permute-start | bytes 2359304 | tf_op jit(solution)/shard_map/ppermute | solution.py:36
  82.9 0.8 fusion.6
  83.7 0.7 fusion.5
  84.4 0.3 copy-done.1
  84.7 1.7 %add_convert_fusion.1 = bf16[512,1024]{1,0:T(8,128)(2,1)} fusion(f32[512,1024]{1,0:T(8,128)S(1)} %fusion.5, bf16[384,512]{1,0:T(8,128)(2,1)S(1)} %bitcast.42, bf16[384,1024]{1,0:T(8,128)(2,1)S(1)} %bitcast.37), kind=kOutput, calls=%fused_computation.1 | convolution fusion | flops 403701760 | bytes 4325376 | tf_op jit(solution)/shard_map/dot_general | solution.py:25
  86.4 1.7 %add_convert_fusion = bf16[1024,512]{1,0:T(8,128)(2,1)} fusion(f32[1024,512]{1,0:T(8,128)S(1)} %fusion.6, bf16[384,1024]{1,0:T(8,128)(2,1)S(1)} %collective-permute-done.2, bf16[384,512]{1,0:T(8,128)(2,1)S(1)} %bitcast.39), kind=kOutput, calls=%fused_computation | convolution fusion | flops 403701760 | bytes 4325376 | tf_op jit(solution)/shard_map/dot_general | solution.py:25
  88.1 0.7 reduce_sum.22
  (25 shorter events, 0.8 us)
Async XLA Ops:
  0.6 1.5 %copy-start = (bf16[1024,512]{1,0:T(8,128)(2,1)S(1)}, bf16[1024,512]{1,0:T(8,128)(2,1)}, u32[]{:S(2)}) copy-start(bf16[1024,512]{1,0:T(8,128)(2,1)} %param.11) | copy-start | bytes 3145732
  0.6 10.9 %copy-start.6 = (s32[48,1024]{1,0:T(8,128)S(1)}, s32[48,1024]{1,0:T(8,128)}, u32[]{:S(2)}) copy-start(s32[48,1024]{1,0:T(8,128)} %param.8) | copy-start | bytes 589828
  0.7 10.9 %copy-start.7 = (f32[48]{0:T(128)S(1)}, f32[48]{0:T(128)}, u32[]{:S(2)}) copy-start(f32[48]{0:T(128)} %param.9) | copy-start | bytes 580
  2.1 10.2 %copy-start.3 = (bf16[768,512]{1,0:T(8,128)(2,1)S(1)}, bf16[768,512]{1,0:T(8,128)(2,1)}, u32[]{:S(2)}) copy-start(bf16[768,512]{1,0:T(8,128)(2,1)} %param.6) | copy-start | bytes 2359300
  2.7 10.7 %collective-permute-start = (bf16[384,1024]{1,0:T(8,128)(2,1)S(1)}, bf16[384,1024]{1,0:T(8,128)(2,1)S(1)}, u32[]{:S(2)}, u32[]{:S(2)}) collective-permute-start(bf16[384,1024]{1,0:T(8,128)(2,1)S(1)} %convolution_convert_fusion), channel_id=1, source_target_pairs={{0,1},{1,0},{2,3},{3,2},{4,5},{5,4},{6,7},{7,6},{8,9},{9,8},{10,11... | collective-permute-start | bytes 2359304 | tf_op jit(solution)/shard_map/ppermute | solution.py:36
  30.1 15.2 %all-to-all-start.1 = ((bf16[8,48,1024]{2,1,0:T(8,128)(2,1)}), bf16[8,48,1024]{2,1,0:T(8,128)(2,1)S(1)}, u32[]{:S(2)}, u32[]{:S(2)}) async-start(bf16[8,48,1024]{2,1,0:T(8,128)(2,1)} %multiply_convert_fusion), calls=%async_computation.1 | async-start | bytes 1572864 | tf_op jit(solution)/shard_map/all_to_all | solution.py:77
  45.2 7.1 %collective-permute-start.1 = (bf16[384,1024]{1,0:T(8,128)(2,1)S(1)}, bf16[384,1024]{1,0:T(8,128)(2,1)S(1)}, u32[]{:S(2)}, u32[]{:S(2)}) collective-permute-start(bf16[384,1024]{1,0:T(8,128)(2,1)S(1)} %bitcast.35), channel_id=1, source_target_pairs={{0,1},{1,0},{2,3},{3,2},{4,5},{5,4},{6,7},{7,6},{8,9},{9,8},{10,11... | collective-permute-start | bytes 2359304 | tf_op jit(solution)/shard_map/ppermute | solution.py:36
  50.4 1.9 %copy-start.8 = (bf16[512,1024]{1,0:T(8,128)(2,1)S(1)}, bf16[512,1024]{1,0:T(8,128)(2,1)}, u32[]{:S(2)}) copy-start(bf16[512,1024]{1,0:T(8,128)(2,1)} %param.10) | copy-start | bytes 3145732
  52.3 0.9 copy-start.4
  54.3 33.8 %all-to-all-start.2 = ((bf16[32,24,512]{2,1,0:T(8,128)(2,1)}), bf16[32,24,512]{2,1,0:T(8,128)(2,1)S(1)}, u32[]{:S(2)}, u32[]{:S(2)}) async-start(bf16[32,24,512]{2,1,0:T(8,128)(2,1)} %bitcast.14), calls=%async_computation.2 | async-start | bytes 1572864 | tf_op jit(solution)/shard_map/all_to_all | solution.py:87
  66.4 17.2 %copy-start.2 = (bf16[8,1,48,512]{3,2,1,0:T(8,128)(2,1)S(1)}, bf16[8,1,48,512]{3,2,1,0:T(8,128)(2,1)}, u32[]{:S(2)}) copy-start(bf16[8,1,48,512]{3,2,1,0:T(8,128)(2,1)} %get-tuple-element.31) | copy-start | bytes 1179652
  66.4 17.2 %copy-start.5 = (bf16[384,1024]{1,0:T(8,128)(2,1)S(1)}, bf16[384,1024]{1,0:T(8,128)(2,1)}, u32[]{:S(2)}) copy-start(bf16[384,1024]{1,0:T(8,128)(2,1)} %copy-done.4) | copy-start | bytes 2359300
  78.3 8.0 %collective-permute-start.2 = (bf16[384,1024]{1,0:T(8,128)(2,1)S(1)}, bf16[384,1024]{1,0:T(8,128)(2,1)S(1)}, u32[]{:S(2)}, u32[]{:S(2)}) collective-permute-start(bf16[384,1024]{1,0:T(8,128)(2,1)S(1)} %all_gather.7), channel_id=1, source_target_pairs={{0,1},{1,0},{2,3},{3,2},{4,5},{5,4},{6,7},{7,6},{8,9},{9,8},{10,11... | collective-permute-start | bytes 2359304 | tf_op jit(solution)/shard_map/ppermute | solution.py:36
  83.7 1.0 %copy-start.1 = (bf16[8,1,48,512]{3,2,1,0:T(8,128)(2,1)S(1)}, bf16[8,1,48,512]{3,2,1,0:T(8,128)(2,1)}, u32[]{:S(2)}) copy-start(bf16[8,1,48,512]{3,2,1,0:T(8,128)(2,1)} %get-tuple-element.32) | copy-start | bytes 1179652
